TPU v7x, 256 devices: a whole 4x4x8 slice. The times are simulated.
256 devices in a mesh: cluster: 32 (over x, y, core), dp: 8 (over z).
Axes of the slice: x: 4, y: 4, z: 8, core: 2. Of those that a mesh axis runs over, the one named last changes fastest.
Arguments:
- hidden_states: bfloat16 [32768, 768], P(('cluster', 'dp')), may hold values from -1.5 to 1.5
- ln_gain: float32 [768], replicated, may hold values from 0.5 to 1.5
- beam_ids: int32 [32768, 8], P(('cluster', 'dp')), may hold values from 0 to 31, all different within a row; in each aligned block of 128 rows (0 to 127, 128 to 255, ...) at most 64 rows name the same one
- positive_ids: int32 [32768, 8], P(('cluster', 'dp')), may hold values from 0 to 4095
- cluster_sizes: int32 [32], P('cluster'), may hold values from 128 to 512
- head_rows: float32 [32, 512, 768], P('cluster'), may hold values from -0.21875 to 0.21875
- first_moment: float32 [32, 512, 768], P('cluster'), may hold values from -3 to 3
- second_moment: float32 [32, 512, 768], P('cluster'), may hold values from 0.01 to 1
Outputs:
- new_head: float32 [32, 512, 768], P('cluster')
- new_first: float32 [32, 512, 768], P('cluster')
- new_second: float32 [32, 512, 768], P('cluster')
- input_grad: bfloat16 [32768, 768], P(('cluster', 'dp'))
- gain_grad: float32 [768], replicated
Inputs may be any that keep to these rules, and one draw needn't show every extreme that they name: `beam_ids`: each row names 8 different clusters. Within the rows of one device no cluster is named by more than 64 rows, and in every draw some cluster is named by exactly 64 rows of some device.
All inputs are finite; a program needn't handle non-finite values.
Results may differ from a plain program's by a relative error of at most 0.025.
Values may be sent and summed in bfloat16 or wider, within the bound.
A program may use at most 128 MiB of HBM per device.

v0:
```python
from functools import partial

import jax
import jax.numpy as jnp
from jax import lax
from jax.sharding import PartitionSpec as P

norm_eps = 1e-05
learn_rate = 0.01
first_decay = 0.9
second_decay = 0.999
adam_eps = 1e-08
second_fix = 0.632304575226


def normalize(hidden_states, ln_gain):
    values = hidden_states.astype(jnp.float32)
    center = jnp.mean(values, axis=1, keepdims=True)
    spread = jnp.mean(jnp.square(values - center), axis=1, keepdims=True)
    inverse = lax.rsqrt(spread + norm_eps)
    normed = (values - center) * inverse
    return (normed, inverse, (normed * ln_gain).astype(jnp.bfloat16))


def norm_backward(emb_grad, normed, inverse, ln_gain):
    scaled = emb_grad * ln_gain
    first_mean = jnp.mean(scaled, axis=1, keepdims=True)
    second_mean = jnp.mean(scaled * normed, axis=1, keepdims=True)
    return ((scaled - first_mean - normed * second_mean) * inverse).astype(jnp.bfloat16)


def adam_update(head_rows, first_moment, second_moment, head_grad):
    new_first = first_decay * first_moment + (1.0 - first_decay) * head_grad
    new_second = second_decay * second_moment + (1.0 - second_decay) * head_grad * head_grad
    step_size = new_first / (jnp.sqrt(new_second / second_fix) + adam_eps)
    return (head_rows - learn_rate * step_size, new_first, new_second)


def place_rows(beam_ids, positive_ids, targets, capacity, labels):
    row_count, beam_width = beam_ids.shape
    target_count = targets.shape[0]
    match = beam_ids[:, None, :] == targets[None, :, None]
    chosen = jnp.any(match, axis=2)
    position = jnp.sum(jnp.where(match, jnp.arange(beam_width, dtype=jnp.int32), 0), axis=2)
    ranks = jnp.cumsum(chosen.astype(jnp.int32), axis=0) - 1
    slot_rows = jnp.where(chosen, ranks, capacity)
    columns = jnp.broadcast_to(
        jnp.arange(target_count, dtype=jnp.int32)[None, :], (row_count, target_count)
    )
    owners = jnp.arange(row_count, dtype=jnp.int32)[:, None]
    sources = (
        jnp.full((target_count, capacity), -1, jnp.int32)
        .at[columns, slot_rows]
        .set(owners, mode="drop")
    )
    offset = positive_ids[:, None, :] - position[:, :, None] * labels
    label_ids = jnp.where((offset >= 0) & (offset < labels), offset, -1)
    by_target = jnp.transpose(label_ids, (1, 0, 2))
    safe_rows = jnp.maximum(sources, 0)
    taken = jnp.take_along_axis(by_target, safe_rows[:, :, None], axis=1)
    slot_labels = jnp.where(sources[:, :, None] >= 0, taken, -1)
    return (sources, slot_labels)


def shards(
    hidden_states,
    ln_gain,
    beam_ids,
    positive_ids,
    cluster_sizes,
    head_rows,
    first_moment,
    second_moment,
):
    row_count, width = hidden_states.shape
    beam_width = beam_ids.shape[1]
    labels = head_rows.shape[1]
    cluster_count = lax.axis_size("cluster")
    capacity = min(row_count, 2 * row_count * beam_width // cluster_count)
    normed, inverse, embedded = normalize(hidden_states, ln_gain)
    group_emb, group_beams, group_pos = (
        lax.all_gather(embedded, "cluster", axis=0, tiled=True),
        lax.all_gather(beam_ids, "cluster", axis=0, tiled=True),
        lax.all_gather(positive_ids, "cluster", axis=0, tiled=True),
    )
    block_emb = group_emb.reshape(cluster_count, row_count, width)
    block_beams = group_beams.reshape(cluster_count, row_count, beam_width)
    block_pos = group_pos.reshape(cluster_count, row_count, group_pos.shape[1])
    own_target = jnp.reshape(lax.axis_index("cluster"), (1,))
    placer = partial(place_rows, targets=own_target, capacity=capacity, labels=labels)
    block_sources, block_labels = jax.vmap(placer)(block_beams, block_pos)
    sources = block_sources[:, 0]
    slot_labels = block_labels[:, 0]
    fetched = jnp.take_along_axis(block_emb, jnp.maximum(sources, 0)[:, :, None], axis=1)
    rows_in = jnp.where(sources[:, :, None] >= 0, fetched, jnp.zeros((), jnp.bfloat16))
    weights = head_rows[0].astype(jnp.bfloat16)
    label_iota = jnp.arange(labels, dtype=jnp.int32)
    live_cols = label_iota[None, :] < cluster_sizes[0]
    flat_rows = rows_in.reshape(-1, width)
    flat_labels = slot_labels.reshape(flat_rows.shape[0], -1)
    slot_total = flat_rows.shape[0]
    block_rows_n = min(slot_total, 1024)
    block_total = slot_total // block_rows_n

    def score_block(running, piece):
        block_rows, block_labels = piece
        logits = jnp.dot(block_rows, weights.T, preferred_element_type=jnp.float32)
        target = jnp.any(block_labels[:, :, None] == label_iota, axis=1).astype(jnp.float32)
        slope = (jnp.where(live_cols, jax.nn.sigmoid(logits) - target, 0.0) / beam_width).astype(
            jnp.bfloat16
        )
        running = running + lax.dot_general(
            slope, block_rows, (((0,), (0,)), ((), ())), preferred_element_type=jnp.float32
        )
        returned = jnp.dot(slope, weights, preferred_element_type=jnp.float32).astype(jnp.bfloat16)
        return (running, returned)

    start_grad = jnp.zeros((labels, width), jnp.float32)
    pieces = (
        flat_rows.reshape(block_total, block_rows_n, width),
        flat_labels.reshape(block_total, block_rows_n, -1),
    )
    head_grad, returned_all = lax.scan(score_block, start_grad, pieces)
    returned_all = returned_all.reshape(cluster_count, capacity, width)
    slot_hits = (sources[:, :, None] == jnp.arange(row_count, dtype=jnp.int32)).astype(jnp.bfloat16)
    row_total = lax.axis_size("cluster") * row_count
    summed = jnp.einsum("scr,scd->srd", slot_hits, returned_all, preferred_element_type=jnp.float32)
    emb_grad = lax.psum_scatter(
        summed.reshape(row_total, width).astype(jnp.bfloat16),
        "cluster",
        scatter_dimension=0,
        tiled=True,
    ).astype(jnp.float32)
    gain_part = jnp.sum(emb_grad * normed, axis=0)
    gain_grad = lax.psum(gain_part, ("cluster", "dp"))
    total_grad = lax.psum(head_grad.astype(jnp.bfloat16), "dp").astype(jnp.float32)
    input_grad = norm_backward(emb_grad, normed, inverse, ln_gain)
    new_head, new_first, new_second = adam_update(
        head_rows[0], first_moment[0], second_moment[0], total_grad
    )
    return (new_head[None], new_first[None], new_second[None], input_grad, gain_grad)


def solution(mesh):
    in_specs = (
        P(("cluster", "dp"), None),
        P(),
        P(("cluster", "dp"), None),
        P(("cluster", "dp"), None),
        P("cluster"),
        P("cluster", None, None),
        P("cluster", None, None),
        P("cluster", None, None),
    )
    out_specs = (
        P("cluster", None, None),
        P("cluster", None, None),
        P("cluster", None, None),
        P(("cluster", "dp"), None),
        P(),
    )
    return jax.shard_map(shards, mesh=mesh, in_specs=in_specs, out_specs=out_specs, check_vma=False)
```

profile of v0, /device:TPU:2, one launch (start us, length us, event | category | flops | bytes accessed | tf_op | source)
XLA Modules:
  0.0 506.5 jit_solution(4215344223486193413)
XLA Ops:
  11.3 24.6 %all_gather.9 = s32[4096,8]{0,1:T(8,128)S(1)} all-gather(s32[128,8]{0,1:T(8,128)} %param.12), channel_id=1, replica_groups=mesh['cluster'=32,'dp'=8] {'cluster'}, dimensions={0}, use_global_device_ids=true | all-gather | bytes 135168 | tf_op jit(solution)/shard_map/all_gather | solution.py:83
  39.6 1.9 compare_select_fusion
  41.5 2.7 copy.48
  44.7 15.5 %scatter_custom_fusion = s32[2048]{0:T(1024)S(1)} fusion(s32[4096]{0:T(1024)S(1)} %bitcast.90, s32[4096]{0:T(1024)S(1)} %iota_bitcast_fusion, s32[]{:T(128)} %constant.46.clone.1), kind=kCustom, calls=%fused_computation.73 | custom fusion | bytes 8196
  60.5 22.5 %all_gather.11 = s32[4096,8]{0,1:T(8,128)S(1)} all-gather(s32[128,8]{0,1:T(8,128)S(1)} %copy-done.6), channel_id=1, replica_groups=mesh['cluster'=32,'dp'=8] {'cluster'}, dimensions={0}, use_global_device_ids=true | all-gather | bytes 135168 | tf_op jit(solution)/shard_map/all_gather | solution.py:84
  83.1 1.9 copy.44
  85.0 4.1 select_bitcast_fusion
  89.1 53.1 %gather_fusion.1 = s32[2048,8]{1,0:T(8,128)} fusion(s32[32,128,8]{2,1,0:T(8,128)} %select_bitcast_fusion, s32[2048]{0:T(1024)S(1)} %reshape.307), kind=kCustom, calls=%fused_computation.1 | custom fusion | bytes 147456 | tf_op jit(solution)/shard_map/vmap(jit(take_along_axis))/gather | solution.py:60
  144.7 65.8 %gather_fusion = bf16[2048,768]{1,0:T(8,128)(2,1)} fusion(bf16[32,128,768]{2,1,0:T(8,128)(2,1)} %bitcast.84, s32[2048]{0:T(1024)S(1)} %reshape.299), kind=kCustom, calls=%fused_computation | custom fusion | bytes 6307840 | tf_op jit(solution)/shard_map/jit(take_along_axis)/gather | solution.py:94
  210.5 3.4 select_select_fusion
  213.9 30.8 %while.14 = (s32[]{:T(128)}, f32[512,768]{1,0:T(8,128)S(1)}, bf16[2,1024,768]{2,1,0:T(8,128)(2,1)}, bf16[2,1024,768]{2,1,0:T(8,128)(2,1)}, bf16[512,768]{1,0:T(8...) while((s32[]{:T(128)}, f32[512,768]{1,0:T(8,128)S(1)}, ...), condition=%wide.region_8.9_spmd.clone.clone, body=%wide.region_6.8_spmd.clone.sunk.clone | while | flops 2429551104 | bytes 16943740 | solution.py:123
  214.1 6.5 %fusion.65 = pred[1024,512]{1,0:T(8,128)(4,1)S(1)} fusion(s32[1024,8]{1,0:T(8,128)S(1)} %copy.51), kind=kLoop, calls=%fused_computation.6.clone.1.clone | loop fusion | flops 7864320 | bytes 557056 | tf_op jit(solution)/shard_map/while/body/eval_jaxpr/reduce_or | solution.py:108
  221.3 3.1 multiply_convert_fusion.3
  224.4 2.1 bitcast_dynamic-update-slice_fusion.3
  226.5 2.7 select_add_fusion.3
  229.5 6.5 %fusion.65 = pred[1024,512]{1,0:T(8,128)(4,1)S(1)} fusion(s32[1024,8]{1,0:T(8,128)S(1)} %copy.51), kind=kLoop, calls=%fused_computation.6.clone.1.clone | loop fusion | flops 7864320 | bytes 557056 | tf_op jit(solution)/shard_map/while/body/eval_jaxpr/reduce_or | solution.py:108
  236.7 3.1 multiply_convert_fusion.3
  239.8 2.2 bitcast_dynamic-update-slice_fusion.3
  242.0 2.7 select_add_fusion.3
  246.1 7.2 %convolution_convert_fusion.1 = bf16[32,128,768]{2,1,0:T(8,128)(2,1)} fusion(bf16[32,64,768]{2,1,0:T(8,128)(2,1)} %bitcast.16, s32[32,64]{1,0:T(8,128)S(1)} %squeeze.20), kind=kOutput, calls=%fused_computation.21 | convolution fusion | flops 406061056 | bytes 9445376 | tf_op jit(solution)/shard_map/scr,scd->srd/dot_general | solution.py:127
  253.3 73.4 %all-reduce.3.cloned.1.call-done = bf16[512,768]{1,0:T(8,128)(2,1)} async-done(((bf16[512,768]{1,0:T(8,128)(2,1)}), bf16[512,768]{1,0:T(8,128)(2,1)}) %all-reduce.3.cloned.1.call-update) | async-done | bytes 786448 | tf_op jit(solution)/shard_map/psum | solution.py:136
  326.7 4.9 fusion.18
  331.6 91.7 %reduce-scatter.2.cloned.1.call-done = bf16[128,768]{1,0:T(8,128)(2,1)} async-done(((bf16[4096,768]{1,0:T(8,128)(2,1)}), bf16[128,768]{1,0:T(8,128)(2,1)}) %reduce-scatter.2.cloned.1.call-update) | async-done | bytes 196624 | tf_op jit(solution)/shard_map/reduce_scatter | solution.py:128
  424.4 73.7 %psum.15 = f32[768]{0:T(1024)} all-reduce(f32[768]{0:T(1024)S(1)} %get-tuple-element.79), channel_id=1, replica_groups=mesh['cluster'=32,'dp'=8] {'cluster','dp'}, use_global_device_ids=true, to_apply=%region_14.15 | all-reduce | flops 768 | bytes 6144 | tf_op jit(solution)/shard_map/psum | solution.py:135
  (72 shorter events, 17.1 us)
Async XLA Ops:
  7.2 137.6 %all-gather.2.cloned.1.call-start = ((), (), s32[]{:S(2)}) async-start(), calls=%async_computation.1 | async-start | bytes 6488064 | tf_op jit(solution)/shard_map/all_gather | solution.py:82
  11.2 315.5 %all-reduce.3.cloned.1.call-start = ((), (), s32[]{:S(2)}) async-start(), calls=%async_computation.2 | async-start | bytes 1572864 | tf_op jit(solution)/shard_map/psum | solution.py:136
  41.5 2.7 copy-start.8
  41.5 2.9 copy-start.7
  41.5 19.0 %copy-start.6 = (s32[128,8]{0,1:T(8,128)S(1)}, s32[128,8]{0,1:T(8,128)}, u32[]{:S(2)}) copy-start(s32[128,8]{0,1:T(8,128)} %param.13) | copy-start | bytes 12292
  89.1 54.6 %copy-start = (f32[1,512,768]{2,1,0:T(8,128)S(1)}, f32[1,512,768]{2,1,0:T(8,128)}, u32[]{:S(2)}) copy-start(f32[1,512,768]{2,1,0:T(8,128)} %param.15) | copy-start | bytes 4718596
  221.3 3.1 copy-start.4
  236.7 3.1 copy-start.4
  245.8 177.5 %reduce-scatter.2.cloned.1.call-start = ((), (), s32[]{:S(2)}) async-start(), calls=%async_computation.3 | async-start | bytes 6488064 | tf_op jit(solution)/shard_map/reduce_scatter | solution.py:128
  253.3 73.4 %copy-start.1 = (f32[1,512,768]{2,1,0:T(8,128)S(1)}, f32[1,512,768]{2,1,0:T(8,128)}, u32[]{:S(2)}) copy-start(f32[1,512,768]{2,1,0:T(8,128)} %param.15) | copy-start | bytes 4718596
  253.3 73.4 %copy-start.3 = (f32[1,512,768]{2,1,0:T(8,128)S(1)}, f32[1,512,768]{2,1,0:T(8,128)}, u32[]{:S(2)}) copy-start(f32[1,512,768]{2,1,0:T(8,128)} %param.17) | copy-start | bytes 4718596
  253.3 170.0 %copy-start.2 = (bf16[128,768]{1,0:T(8,128)(2,1)S(1)}, bf16[128,768]{1,0:T(8,128)(2,1)}, u32[]{:S(2)}) copy-start(bf16[128,768]{1,0:T(8,128)(2,1)} %param.10) | copy-start | bytes 589828
  253.3 169.9 %copy-start.5 = (f32[768]{0:T(1024)S(1)}, f32[768]{0:T(1024)}, u32[]{:S(2)}) copy-start(f32[768]{0:T(1024)} %param.11) | copy-start | bytes 9220
Sparse Core Ops, SparseCore 0:
  11.3 56.3 all-gather.1
  245.9 80.7 all-reduce.2
  331.3 91.9 reduce-scatter.1
where the time goes:
time: 512 us; the launch traced here: 506 us
  waiting for transfers between devices  165 us (32%)
  local copies, waits for them, and re-layouts  145 us (28%)
  blocking collectives  121 us (24%)
  other arithmetic  37.8 us (7%)
  matrix products  23.1 us (5%)
  between operations  13.9 us (3%)
    reduce_scatter x1, waiting for transfers between devices, shards(): lax.psum_scatter(summed.reshape(row_total, width).astype(jnp.bfloat16), '...  91.7 us
    psum x1, blocking collectives, shards(): gain_grad = lax.psum(gain_part, ('cluster', 'dp'))  73.7 us
    psum x1, waiting for transfers between devices, shards(): lax.psum(head_grad.astype(jnp.bfloat16), 'dp').astype(jnp.float32)  73.4 us
    gather x2, local copies, waits for them, and re-layouts, shards(): jnp.take_along_axis(block_emb, jnp.maximum(sources, 0)[:, :, None], axis=1)  65.9 us
    gather x3, local copies, waits for them, and re-layouts, place_rows(): taken = jnp.take_along_axis(by_target, safe_rows[:, :, None], axis=1)  54.6 us
    all_gather x1, blocking collectives, shards(): lax.all_gather(beam_ids, 'cluster', axis=0, tiled=True)  24.6 us
    all_gather x1, blocking collectives, shards(): lax.all_gather(positive_ids, 'cluster', axis=0, tiled=True)  22.5 us
    unnamed x22, local copies, waits for them, and re-layouts  18.5 us
  transfers between devices with their start and end apart: 3, of which 2 were waited for; matrix products, arithmetic and copies ran while one was open for 19% of the time, Pallas kernels for 0%

commit v1 on v0

v1 whole, which is shorter than its diff:
```python
import functools

import jax
import jax.numpy as jnp
from jax import lax
from jax.experimental import pallas as pl
from jax.experimental.pallas import tpu as pltpu
from jax.sharding import PartitionSpec as P

MESH = pl.DeviceIdType.MESH
F32 = jnp.float32
BF16 = jnp.bfloat16

norm_eps = 1e-05
learn_rate = 0.01
first_decay = 0.9
second_decay = 0.999
adam_eps = 1e-08
second_fix = 0.632304575226

SIDE = 4
PLANE = 32
CHIPS = (
    (0, 0), (1, 0), (0, 1), (3, 0), (0, 3), (2, 0), (0, 2), (1, 1),
    (3, 3), (1, 3), (3, 1), (2, 1), (1, 2), (2, 3), (3, 2), (2, 2),
)


def table_at(values, at):
    half = len(values) // 2
    low = sum(v * 4**i for i, v in enumerate(values[:half]))
    high = sum(v * 4**i for i, v in enumerate(values[half:]))
    above = at // half
    word = low + above * (high - low)
    return lax.rem(lax.shift_right_logical(word, 2 * lax.rem(at, half)), 4)


def kernel(
    hid_ref, gain_ref, ids_ref, size_ref, head_ref,
    hg_ref, igrad_ref, ggrad_ref,
    emb, ids, wh, wt, hg, part, from_core, half_in, quart_in, half_in2, quart_in2,
    hgb, hgf, zq, zh, gplane, gz, egrad,
    ids_sem, ag_send, ag_recv, core_recv,
    rs_send, rs_core, rs_h, rs_q, rs_h2, rs_q2,
    z_send, z_q, z_h, zg_send, zg, g_sem,
):
    c = lax.axis_index("cluster")
    z = lax.axis_index("dp")
    depth = lax.axis_size("dp")
    rows, width = hid_ref.shape
    labels = head_ref.shape[0]
    beam = 8
    x, y, k = c // (2 * SIDE), lax.rem(c // 2, SIDE), lax.rem(c, 2)
    sibling = (c + 1 - 2 * k, z)

    def chip(dx, dy):
        return lax.rem(x + dx, SIDE) * SIDE + lax.rem(y + dy, SIDE)

    def chip_t(t, du, dv):
        return chip(du, dv) if t == 0 else chip(dv, du)

    def peer_t(t, du, dv):
        return (2 * chip_t(t, du, dv) + k, z)

    def copy(src, dst, send, recv, dev):
        return pltpu.make_async_remote_copy(
            src_ref=src, dst_ref=dst, send_sem=send, recv_sem=recv, device_id=dev, device_id_type=MESH
        )

    def arrived(dst, recv):
        copy(dst, dst, recv, recv, sibling).wait_recv()

    def sent(src, send):
        copy(src, src, send, send, sibling).wait_send()

    barrier = pltpu.get_barrier_semaphore()

    def greet(i, _):
        pl.semaphore_signal(barrier, inc=1, device_id=(lax.rem(c + i, PLANE), z), device_id_type=MESH)
        return _

    def greet_z(i, _):
        pl.semaphore_signal(barrier, inc=1, device_id=(c, lax.rem(z + i, depth)), device_id_type=MESH)
        return _

    lax.fori_loop(1, PLANE, greet, 0)
    lax.fori_loop(1, depth, greet_z, 0)

    values = hid_ref[...].astype(F32)
    center = jnp.mean(values, axis=1, keepdims=True)
    spread = jnp.mean(jnp.square(values - center), axis=1, keepdims=True)
    normed = (values - center) * lax.rsqrt(spread + norm_eps)
    emb[c] = (normed * gain_ref[...]).astype(BF16)
    ids[c] = ids_ref[...]
    pl.semaphore_wait(barrier, PLANE - 1 + depth - 1)

    half, quart = rows // 2, rows // 4

    def event(dx, dy):
        src = 2 * chip(dx, dy) + k
        for t in range(2):
            du, dv = (dx, dy) if t == 0 else (dy, dx)
            whole = emb.at[src, pl.ds(t * half, half)]
            q = [emb.at[src, pl.ds(t * half + i * quart, quart)] for i in range(2)]
            if (dx, dy) != (0, 0):
                arrived(whole, ag_recv.at[t, du, dv])

            def push(ref, tu, tv, t=t, du=du, dv=dv):
                there = ag_recv.at[t, (du - tu) % SIDE, (dv - tv) % SIDE]
                copy(ref, ref, ag_send, there, peer_t(t, tu % SIDE, tv % SIDE)).start()

            if dv == 0:
                if du == 0:
                    push(whole, 1, 0)
                    push(whole, -1, 0)
                elif du == 3:
                    push(q[0], 1, 0)
                elif du == 1:
                    push(q[1], -1, 0)
                push(whole, 0, 1)
                push(whole, 0, -1)
            elif dv == 3:
                push(q[0], 0, 1)
            elif dv == 1:
                push(q[1], 0, -1)
        copy(emb.at[src], emb.at[src], ag_send, core_recv.at[dx, dy], sibling).start()

    def send_ids(i, _):
        copy(ids.at[c], ids.at[c], ids_sem.at[0], ids_sem.at[1], (lax.rem(c + i, PLANE), z)).start()
        return _

    event(0, 0)
    lax.fori_loop(1, PLANE, send_ids, 0)

    wh[...] = (head_ref[...].astype(BF16) * 0.5).astype(BF16)
    for i in range(width // 128):
        cols = pl.ds(i * 128, 128)
        wt[cols, :] = head_ref[:, cols].T.astype(BF16)
    hg[...] = jnp.zeros_like(hg)
    size = size_ref[0]
    arrived(ids.at[pl.ds(0, PLANE - 1)], ids_sem.at[1])

    def compute(at):
        dx, dy = table_at([p[0] for p in CHIPS], at), table_at([p[1] for p in CHIPS], at)
        ch = chip(dx, dy)
        arrived(emb.at[2 * ch + 1 - k], core_recv.at[dx, dy])
        block = emb[pl.ds(2 * ch, 2)].reshape(2 * rows, width)
        label, limit = [], []
        for s in range(2):
            own = ids[2 * ch + s].astype(jnp.int32)
            match = own[0:beam] == c
            place = lax.broadcasted_iota(jnp.int32, (beam, rows), 0)
            place = jnp.sum(jnp.where(match, place, 0), axis=0, keepdims=True)
            chosen = jnp.max(jnp.where(match, 1, 0), axis=0, keepdims=True)
            label.append(own[beam:] - place * labels)
            limit.append(chosen * size)
        label = jnp.concatenate(label, axis=1)
        limit = jnp.concatenate(limit, axis=1)
        logits = lax.dot_general(wh[...], block, (((1,), (1,)), ((), ())), preferred_element_type=F32)
        slot = lax.broadcasted_iota(jnp.int32, (labels, 2 * rows), 0)
        hit = label[0:1] == slot
        for p in range(1, label.shape[0]):
            hit = hit | (label[p : p + 1] == slot)
        step = 0.5 / beam
        slope = step * jnp.tanh(logits) + jnp.where(hit, -step, step)
        slope = jnp.where(slot < limit, slope, 0.0).astype(BF16)
        hg[...] += jnp.dot(slope, block, preferred_element_type=F32)
        back = jnp.dot(wt[...], slope, preferred_element_type=F32).astype(BF16)
        part[2 * ch] = back[:, :rows]
        part[2 * ch + 1] = back[:, rows:]
        there = 2 * ch + 1 - k
        copy(part.at[there], from_core.at[ch], rs_send, rs_core.at[dx, dy], sibling).start()

    def join(at):
        dx, dy = table_at([p[0] for p in CHIPS], at), table_at([p[1] for p in CHIPS], at)
        ch = chip(dx, dy)
        arrived(from_core.at[ch], rs_core.at[dx, dy])
        part[2 * ch + k] += from_core[ch]

    count = len(CHIPS)

    def turn(e, _):
        for i in range(1, count):
            pl.when(e == i)(functools.partial(event, *CHIPS[i]))

        @pl.when((e >= 1) & (e <= count))
        def _compute():
            compute(e - 1)

        @pl.when(e >= 2)
        def _join():
            join(e - 2)

        return _

    lax.fori_loop(1, count + 2, turn, 0)

    piece = labels // depth
    far = depth // 2

    def at_z(i):
        return lax.rem(z + i + depth, depth)

    def rows_z(i, lo=0, n=piece):
        return pl.ds(pl.multiple_of(at_z(i) * piece + lo, piece // 2), n)

    hgb[...] = hg[...].astype(BF16)

    def z_first():
        for s in range(2):
            lo = s * (piece // 2)
            src = hgb.at[rows_z(far, lo, piece // 2)]
            copy(src, zq.at[s], z_send, z_q.at[s], (c, at_z(1 - 2 * s))).start()

    def z_next(i):
        for s in range(2):
            way = 1 - 2 * s
            own = rows_z(way * (far - 1 - i))
            if i == 0:
                arrived(zq.at[s], z_q.at[s])
                mid = rows_z(way * (far - 1), s * (piece // 2), piece // 2)
                hgb[mid] += zq[s]
            else:
                arrived(zh.at[s, i - 1], z_h.at[s, i - 1])
                hgb[own] += zh[s, i - 1]
            copy(hgb.at[own], zh.at[s, i], z_send, z_h.at[s, i], (c, at_z(way))).start()

    def z_last():
        total = hgb[rows_z(0)].astype(F32)
        for s in range(2):
            arrived(zh.at[s, far - 2], z_h.at[s, far - 2])
            total += zh[s, far - 2].astype(F32)
        hgf[rows_z(0)] = total.astype(BF16)
        for s in range(2):
            own = hgf.at[rows_z(0)]
            copy(own, own, zg_send, zg.at[s, 0], (c, at_z(1 - 2 * s))).start()

    def z_spread(i):
        for s in range(2):
            way = 1 - 2 * s
            own = hgf.at[rows_z(-way * i)]
            arrived(own, zg.at[s, i - 1])
            if i == far - 1:
                own = hgf.at[rows_z(-way * i, s * (piece // 2), piece // 2)]
            copy(own, own, zg_send, zg.at[s, i], (c, at_z(way))).start()

    def z_end():
        for s in range(2):
            arrived(hgf.at[rows_z(far, s * (piece // 2), piece // 2)], zg.at[s, far - 1])

    fh, fq = width // 2, width // 4

    def feats(t, lo, n):
        return pl.ds(t * fh + lo, n)

    def dest(t, du, dv):
        return 2 * chip_t(t, du % SIDE, dv % SIDE) + k

    def v_first(t, du):
        for s in range(2):
            src = part.at[dest(t, du, 2), feats(t, s * fq, fq)]
            copy(src, quart_in.at[t, du, s], rs_send, rs_q.at[t, du, s], peer_t(t, 0, (1, 3)[s])).start()

    def v_next(t, du):
        for s in range(2):
            arrived(quart_in.at[t, du, s], rs_q.at[t, du, s])
            to = dest(t, du, (1, 3)[s])
            part[to, feats(t, s * fq, fq)] += quart_in[t, du, s]
            src = part.at[to, feats(t, 0, fh)]
            copy(src, half_in.at[t, du, s], rs_send, rs_h.at[t, du, s], peer_t(t, 0, (1, 3)[s])).start()

    def v_last(t, du):
        to = dest(t, du, 0)
        for s in range(2):
            arrived(half_in.at[t, du, s], rs_h.at[t, du, s])
        total = part[to, feats(t, 0, fh)].astype(F32)
        total += half_in[t, du, 0].astype(F32) + half_in[t, du, 1].astype(F32)
        part[to, feats(t, 0, fh)] = total.astype(BF16)

    def u_first(t):
        for s in range(2):
            src = part.at[dest(t, 2, 0), feats(t, s * fq, fq)]
            copy(src, quart_in2.at[t, s], rs_send, rs_q2.at[t, s], peer_t(t, (1, 3)[s], 0)).start()

    def u_next(t):
        for s in range(2):
            arrived(quart_in2.at[t, s], rs_q2.at[t, s])
            to = dest(t, (1, 3)[s], 0)
            part[to, feats(t, s * fq, fq)] += quart_in2[t, s]
            src = part.at[to, feats(t, 0, fh)]
            copy(src, half_in2.at[t, s], rs_send, rs_h2.at[t, s], peer_t(t, (1, 3)[s], 0)).start()

    def u_last(t):
        for s in range(2):
            arrived(half_in2.at[t, s], rs_h2.at[t, s])
        total = part[c, feats(t, 0, fh)].astype(F32)
        total += half_in2[t, 0].astype(F32) + half_in2[t, 1].astype(F32)
        egrad[feats(t, 0, fh), :] = total

    def g_first():
        total = jnp.sum(wh[...].astype(F32) * hg[...], axis=0, keepdims=True)
        gplane[c] = total * 2.0

        def send(i, _):
            to = (lax.rem(c + i, PLANE), z)
            copy(gplane.at[c], gplane.at[c], g_sem.at[0], g_sem.at[1], to).start()
            return _

        lax.fori_loop(1, PLANE, send, 0)

    def g_next():
        arrived(gplane.at[pl.ds(0, PLANE - 1)], g_sem.at[1])
        gz[z] = jnp.sum(gplane[...], axis=0)

        def send(i, _):
            copy(gz.at[z], gz.at[z], g_sem.at[2], g_sem.at[3], (c, at_z(i))).start()
            return _

        lax.fori_loop(1, depth, send, 0)

    def g_last():
        arrived(gz.at[pl.ds(0, depth - 1)], g_sem.at[3])
        ggrad_ref[...] = jnp.sum(gz[...], axis=0) / gain_ref[...]

    z_first()
    for du in (2, 1, 3, 0):
        for t in range(2):
            v_first(t, du)
    g_first()
    z_next(0)
    for t in range(2):
        v_next(t, 2)
    z_next(1)
    for du in (1, 3):
        for t in range(2):
            v_next(t, du)
    z_next(2)
    for t in range(2):
        v_next(t, 0)
    for t in range(2):
        v_last(t, 2)
        u_first(t)
    z_last()
    for du in (1, 3):
        for t in range(2):
            v_last(t, du)
    for t in range(2):
        u_next(t)
    z_spread(1)
    g_next()
    for t in range(2):
        v_last(t, 0)
    z_spread(2)
    for t in range(2):
        u_last(t)
    z_spread(3)

    emb_grad = egrad[...].T
    values = hid_ref[...].astype(F32)
    center = jnp.mean(values, axis=1, keepdims=True)
    spread = jnp.mean(jnp.square(values - center), axis=1, keepdims=True)
    inverse = lax.rsqrt(spread + norm_eps)
    normed = (values - center) * inverse
    scaled = emb_grad * gain_ref[...]
    first_mean = jnp.mean(scaled, axis=1, keepdims=True)
    second_mean = jnp.mean(scaled * normed, axis=1, keepdims=True)
    igrad_ref[...] = ((scaled - first_mean - normed * second_mean) * inverse).astype(BF16)

    g_last()
    z_end()
    hg_ref[...] = hgf[...]

    sent(emb.at[pl.ds(0, PLANE - 1)], ag_send)
    sent(part.at[pl.ds(0, PLANE - 1)], rs_send)
    sent(ids.at[pl.ds(0, PLANE - 1)], ids_sem.at[0])
    sent(gplane.at[pl.ds(0, PLANE - 1)], g_sem.at[0])
    sent(gz.at[pl.ds(0, depth - 1)], g_sem.at[2])
    sent(hgb.at[pl.ds(0, labels - piece)], z_send)
    sent(hgf.at[pl.ds(0, labels - piece)], zg_send)


def adam_update(head_rows, first_moment, second_moment, head_grad):
    new_first = first_decay * first_moment + (1.0 - first_decay) * head_grad
    new_second = second_decay * second_moment + (1.0 - second_decay) * head_grad * head_grad
    step_size = new_first / (jnp.sqrt(new_second / second_fix) + adam_eps)
    return (head_rows - learn_rate * step_size, new_first, new_second)


def shards(
    hidden_states,
    ln_gain,
    beam_ids,
    positive_ids,
    cluster_sizes,
    head_rows,
    first_moment,
    second_moment,
):
    rows, width = hidden_states.shape
    labels = head_rows.shape[1]
    depth = lax.axis_size("dp")
    ids = jnp.concatenate([beam_ids.T, positive_ids.T], axis=0).astype(jnp.int16)
    vmem = pl.BlockSpec(memory_space=pltpu.VMEM)
    smem = pl.BlockSpec(memory_space=pltpu.SMEM)
    fh, fq, piece, far = width // 2, width // 4, labels // depth, depth // 2
    dma = pltpu.SemaphoreType.DMA
    head_grad, input_grad, gain_grad = pl.pallas_call(
        kernel,
        out_shape=(
            jax.ShapeDtypeStruct((labels, width), BF16),
            jax.ShapeDtypeStruct((rows, width), BF16),
            jax.ShapeDtypeStruct((1, width), F32),
        ),
        in_specs=[vmem, vmem, vmem, smem, vmem],
        out_specs=(vmem, vmem, vmem),
        scratch_shapes=[
            pltpu.VMEM((PLANE, rows, width), BF16),
            pltpu.VMEM((PLANE, 16, rows), jnp.int16),
            pltpu.VMEM((labels, width), BF16),
            pltpu.VMEM((width, labels), BF16),
            pltpu.VMEM((labels, width), F32),
            pltpu.VMEM((PLANE, width, rows), BF16),
            pltpu.VMEM((PLANE // 2, width, rows), BF16),
            pltpu.VMEM((2, SIDE, 2, fh, rows), BF16),
            pltpu.VMEM((2, SIDE, 2, fq, rows), BF16),
            pltpu.VMEM((2, 2, fh, rows), BF16),
            pltpu.VMEM((2, 2, fq, rows), BF16),
            pltpu.VMEM((labels, width), BF16),
            pltpu.VMEM((labels, width), BF16),
            pltpu.VMEM((2, piece // 2, width), BF16),
            pltpu.VMEM((2, far - 1, piece, width), BF16),
            pltpu.VMEM((PLANE, 1, width), F32),
            pltpu.VMEM((depth, 1, width), F32),
            pltpu.VMEM((width, rows), F32),
            dma((2,)),
            dma,
            dma((2, SIDE, SIDE)),
            dma((SIDE, SIDE)),
            dma,
            dma((SIDE, SIDE)),
            dma((2, SIDE, 2)),
            dma((2, SIDE, 2)),
            dma((2, 2)),
            dma((2, 2)),
            dma,
            dma((2,)),
            dma((2, far - 1)),
            dma,
            dma((2, far)),
            dma((4,)),
        ],
        compiler_params=pltpu.CompilerParams(
            collective_id=0, has_side_effects=True, vmem_limit_bytes=56 * 1024 * 1024
        ),
    )(hidden_states, ln_gain[None, :], ids, cluster_sizes, head_rows[0])
    new_head, new_first, new_second = adam_update(
        head_rows[0], first_moment[0], second_moment[0], head_grad.astype(F32)
    )
    return (new_head[None], new_first[None], new_second[None], input_grad, gain_grad[0])


def solution(mesh):
    in_specs = (
        P(("cluster", "dp"), None),
        P(),
        P(("cluster", "dp"), None),
        P(("cluster", "dp"), None),
        P("cluster"),
        P("cluster", None, None),
        P("cluster", None, None),
        P("cluster", None, None),
    )
    out_specs = (
        P("cluster", None, None),
        P("cluster", None, None),
        P("cluster", None, None),
        P(("cluster", "dp"), None),
        P(),
    )
    return jax.shard_map(shards, mesh=mesh, in_specs=in_specs, out_specs=out_specs, check_vma=False)
```

time: 512 us -> 101 us (0.20); the launches traced: 506 us -> 101 us
  waiting for transfers between devices: 165 us -> 0 us
  local copies, waits for them, and re-layouts: 145 us -> 1.96 us
  blocking collectives: 121 us -> 0 us
  Pallas kernels: 0 us -> 90.6 us
  other arithmetic: 37.8 us -> 7.42 us
  matrix products: 23.1 us -> 0 us
  between operations: 13.9 us -> 1.33 us
    gather x5 -> x0, local copies, waits for them, and re-layouts: 121 us -> none  [the longest x2 65.9 us: shards(): jnp.take_along_axis(block_emb, jnp.maximum(sources, 0)[:, :, None], axis=1)]
    reduce_scatter x1 -> x0, waiting for transfers between devices: 91.7 us -> none  [shards(): lax.psum_scatter(summed.reshape(row_total, width).astype(jnp.bfloat16), '...]
    pallas_call x0 -> x1, Pallas kernels: none -> 90.6 us  [shards(): pl.pallas_call(kernel, out_shape=(jax.ShapeDtypeStruct((labels, width), B...]
    psum x1 -> x0, blocking collectives: 73.7 us -> none  [shards(): gain_grad = lax.psum(gain_part, ('cluster', 'dp'))]
    psum x1 -> x0, waiting for transfers between devices: 73.4 us -> none  [shards(): lax.psum(head_grad.astype(jnp.bfloat16), 'dp').astype(jnp.float32)]
    all_gather x2 -> x0, blocking collectives: 47.1 us -> none  [the longest x1 24.6 us: shards(): lax.all_gather(beam_ids, 'cluster', axis=0, tiled=True)]
    dot_general x7 -> x0, matrix products: 23.1 us -> none  [the longest x1 7.17 us: shards(): jnp.einsum('scr,scd->srd', slot_hits, returned_all, preferred_element_typ...]
    unnamed x22 -> x7, local copies, waits for them, and re-layouts: 18.5 us -> 0.69 us
  transfers between devices with their start and end apart: 3 -> 0, of which waited for: 2 -> 0; matrix products, arithmetic and copies ran while one was open for 19% -> 0% of each run, Pallas kernels for 0% -> 0%
where the time goes in v1:
time: 101 us
  Pallas kernels  90.6 us (90%)
  other arithmetic  7.42 us (7%)
  local copies, waits for them, and re-layouts  1.96 us (2%)
  between operations  1.33 us (1%)
    pallas_call x1, Pallas kernels, shards(): pl.pallas_call(kernel, out_shape=(jax.ShapeDtypeStruct((labels, width), B...  90.6 us
    broadcast_in_dim x1, other arithmetic, shards(): new_second[None]  5.39 us

profile of v1, /device:TPU:2, one launch (start us, length us, event | category | flops | bytes accessed | tf_op | source)
XLA Modules:
  0.0 101.3 jit_solution(12409757649366107753)
XLA Ops:
  0.6 0.0 copy-start
  0.6 0.8 convert_bitcast_fusion
  1.5 0.6 pad_add_fusion.ids_ref
  2.1 1.3 %broadcast_in_dim.12.gain_ref = f32[1,768]{1,0:T(1,128)} reshape(f32[768]{0:T(1024)} %param.9) | data formatting | bytes 6144 | tf_op jit(solution)/shard_map/broadcast_in_dim | solution.py:455
  4.0 90.6 %shard_map.119 = (bf16[512,768]{1,0:T(8,128)(2,1)}, bf16[128,768]{1,0:T(8,128)(2,1)}, f32[1,768]{1,0:T(1,128)}) custom-call(bf16[128,768]{1,0:T(8,128)(2,1)} %hid_ref.1, f32[1,768]{1,0:T(1,128)} %broadcast_in_dim.12.gain_ref, s16[16,128]{1,0:T(8,128)(2,1)} %pad_add_fusion.ids_ref, s32[1]{0:T(128)S(6)} %copy.14.size_ref, f32[512,768]{1,0:T(8,128)} %bitcast.24), custom_call_target="tpu_custom_call" | custom-call | tf_op jit(solution)/shard_map/pallas_call | solution.py:407
  94.6 0.0 copy-done
  94.6 0.0 copy-start.2
  94.6 0.0 copy-start.1
  94.6 5.4 %fusion.3 = (f32[1,512,768]{2,1,0:T(8,128)}, f32[1,512,768]{2,1,0:T(8,128)}, f32[1,512,768]{2,1,0:T(8,128)}) fusion(bf16[512,768]{1,0:T(8,128)(2,1)} %get-tuple-element.8, f32[1,512,768]{2,1,0:T(8,128)} %param.15, f32[1,512,768]{2,1,0:T(8,128)} %param.14, f32[1,512,768]{2,1,0:T(8,128)S(1)} %copy-done), kind=kLoop, calls=%fused_computation.6 | loop fusion | flops 5111808 | bytes 10223616 | tf_op jit(solution)/shard_map/broadcast_in_dim | solution.py:459
  100.0 0.0 copy-done.2
  100.0 0.6 reduce
  100.6 0.0 copy-done.1
  100.6 0.7 copy.15
Async XLA Ops:
  0.6 94.0 %copy-start = (f32[1,512,768]{2,1,0:T(8,128)S(1)}, f32[1,512,768]{2,1,0:T(8,128)}, u32[]{:S(2)}) copy-start(f32[1,512,768]{2,1,0:T(8,128)} %param.13) | copy-start | bytes 4718596
  94.6 5.4 %copy-start.2 = (f32[1,768]{1,0:T(1,128)S(1)}, f32[1,768]{1,0:T(1,128)}, u32[]{:S(2)}) copy-start(f32[1,768]{1,0:T(1,128)} %get-tuple-element.10) | copy-start | bytes 9220
  94.6 6.0 %copy-start.1 = (bf16[128,768]{1,0:T(8,128)(2,1)S(1)}, bf16[128,768]{1,0:T(8,128)(2,1)}, u32[]{:S(2)}) copy-start(bf16[128,768]{1,0:T(8,128)(2,1)} %get-tuple-element.24) | copy-start | bytes 589828

commit v2 on v1

--- a/solution.py
+++ b/solution.py
@@ -20,6 +20,7 @@
 
 SIDE = 4
 PLANE = 32
+ZC = 2
 CHIPS = (
     (0, 0), (1, 0), (0, 1), (3, 0), (0, 3), (2, 0), (0, 2), (1, 1),
     (3, 3), (1, 3), (3, 1), (2, 1), (1, 2), (2, 3), (3, 2), (2, 2),
@@ -36,7 +37,7 @@
 
 
 def kernel(
-    hid_ref, gain_ref, ids_ref, size_ref, head_ref,
+    hid_ref, gain_ref, beam_ref, pos_ref, size_ref, head_ref,
     hg_ref, igrad_ref, ggrad_ref,
     emb, ids, wh, wt, hg, part, from_core, half_in, quart_in, half_in2, quart_in2,
     hgb, hgf, zq, zh, gplane, gz, egrad,
@@ -86,13 +87,21 @@
     lax.fori_loop(1, PLANE, greet, 0)
     lax.fori_loop(1, depth, greet_z, 0)
 
+    ids[c] = jnp.concatenate([beam_ref[...], pos_ref[...]], axis=0).astype(jnp.int16)
+    pl.semaphore_wait(barrier, PLANE - 1 + depth - 1)
+
+    def send_ids(i, _):
+        copy(ids.at[c], ids.at[c], ids_sem.at[0], ids_sem.at[1], (lax.rem(c + i, PLANE), z)).start()
+        return _
+
+    lax.fori_loop(1, PLANE, send_ids, 0)
+
     values = hid_ref[...].astype(F32)
     center = jnp.mean(values, axis=1, keepdims=True)
     spread = jnp.mean(jnp.square(values - center), axis=1, keepdims=True)
     normed = (values - center) * lax.rsqrt(spread + norm_eps)
-    emb[c] = (normed * gain_ref[...]).astype(BF16)
-    ids[c] = ids_ref[...]
-    pl.semaphore_wait(barrier, PLANE - 1 + depth - 1)
+    gain = gain_ref[...].reshape(1, width)
+    emb[c] = (normed * gain).astype(BF16)
 
     half, quart = rows // 2, rows // 4
 
@@ -125,12 +134,7 @@
                 push(q[1], 0, -1)
         copy(emb.at[src], emb.at[src], ag_send, core_recv.at[dx, dy], sibling).start()
 
-    def send_ids(i, _):
-        copy(ids.at[c], ids.at[c], ids_sem.at[0], ids_sem.at[1], (lax.rem(c + i, PLANE), z)).start()
-        return _
-
     event(0, 0)
-    lax.fori_loop(1, PLANE, send_ids, 0)
 
     wh[...] = (head_ref[...].astype(BF16) * 0.5).astype(BF16)
     for i in range(width // 128):
@@ -158,9 +162,14 @@
         limit = jnp.concatenate(limit, axis=1)
         logits = lax.dot_general(wh[...], block, (((1,), (1,)), ((), ())), preferred_element_type=F32)
         slot = lax.broadcasted_iota(jnp.int32, (labels, 2 * rows), 0)
-        hit = label[0:1] == slot
-        for p in range(1, label.shape[0]):
-            hit = hit | (label[p : p + 1] == slot)
+        word = lax.shift_right_arithmetic(label, 5)
+        bit = lax.shift_left(jnp.ones_like(label), label & 31)
+        words = lax.broadcasted_iota(jnp.int32, (labels // 32, 2 * rows), 0)
+        bits = jnp.zeros_like(words)
+        for p in range(label.shape[0]):
+            bits = bits | jnp.where(word[p : p + 1] == words, bit[p : p + 1], 0)
+        bits = jnp.broadcast_to(bits[:, None, :], (labels // 32, 32, 2 * rows)).reshape(labels, 2 * rows)
+        hit = lax.shift_left(bits, 31 - (slot & 31)) < 0
         step = 0.5 / beam
         slope = step * jnp.tanh(logits) + jnp.where(hit, -step, step)
         slope = jnp.where(slot < limit, slope, 0.0).astype(BF16)
@@ -201,52 +210,54 @@
     def at_z(i):
         return lax.rem(z + i + depth, depth)
 
-    def rows_z(i, lo=0, n=piece):
-        return pl.ds(pl.multiple_of(at_z(i) * piece + lo, piece // 2), n)
+    chunk = piece // ZC
+    part_z = chunk // 2
+
+    def rows_z(h, i, lo=0, n=chunk):
+        return pl.ds(pl.multiple_of(at_z(i) * piece + h * chunk + lo, part_z), n)
 
     hgb[...] = hg[...].astype(BF16)
 
-    def z_first():
-        for s in range(2):
-            lo = s * (piece // 2)
-            src = hgb.at[rows_z(far, lo, piece // 2)]
-            copy(src, zq.at[s], z_send, z_q.at[s], (c, at_z(1 - 2 * s))).start()
-
-    def z_next(i):
+    def z_first(h):
+        for s in range(2):
+            src = hgb.at[rows_z(h, far, s * part_z, part_z)]
+            copy(src, zq.at[h, s], z_send, z_q.at[h, s], (c, at_z(1 - 2 * s))).start()
+
+    def z_next(h, i):
         for s in range(2):
             way = 1 - 2 * s
-            own = rows_z(way * (far - 1 - i))
+            own = rows_z(h, way * (far - 1 - i))
             if i == 0:
-                arrived(zq.at[s], z_q.at[s])
-                mid = rows_z(way * (far - 1), s * (piece // 2), piece // 2)
-                hgb[mid] += zq[s]
+                arrived(zq.at[h, s], z_q.at[h, s])
+                mid = rows_z(h, way * (far - 1), s * part_z, part_z)
+                hgb[mid] += zq[h, s]
             else:
-                arrived(zh.at[s, i - 1], z_h.at[s, i - 1])
-                hgb[own] += zh[s, i - 1]
-            copy(hgb.at[own], zh.at[s, i], z_send, z_h.at[s, i], (c, at_z(way))).start()
-
-    def z_last():
-        total = hgb[rows_z(0)].astype(F32)
-        for s in range(2):
-            arrived(zh.at[s, far - 2], z_h.at[s, far - 2])
-            total += zh[s, far - 2].astype(F32)
-        hgf[rows_z(0)] = total.astype(BF16)
-        for s in range(2):
-            own = hgf.at[rows_z(0)]
-            copy(own, own, zg_send, zg.at[s, 0], (c, at_z(1 - 2 * s))).start()
-
-    def z_spread(i):
+                arrived(zh.at[h, s, i - 1], z_h.at[h, s, i - 1])
+                hgb[own] += zh[h, s, i - 1]
+            copy(hgb.at[own], zh.at[h, s, i], z_send, z_h.at[h, s, i], (c, at_z(way))).start()
+
+    def z_last(h):
+        total = hgb[rows_z(h, 0)].astype(F32)
+        for s in range(2):
+            arrived(zh.at[h, s, far - 2], z_h.at[h, s, far - 2])
+            total += zh[h, s, far - 2].astype(F32)
+        hgf[rows_z(h, 0)] = total.astype(BF16)
+        for s in range(2):
+            own = hgf.at[rows_z(h, 0)]
+            copy(own, own, zg_send, zg.at[h, s, 0], (c, at_z(1 - 2 * s))).start()
+
+    def z_spread(h, i):
         for s in range(2):
             way = 1 - 2 * s
-            own = hgf.at[rows_z(-way * i)]
-            arrived(own, zg.at[s, i - 1])
+            own = hgf.at[rows_z(h, -way * i)]
+            arrived(own, zg.at[h, s, i - 1])
             if i == far - 1:
-                own = hgf.at[rows_z(-way * i, s * (piece // 2), piece // 2)]
-            copy(own, own, zg_send, zg.at[s, i], (c, at_z(way))).start()
-
-    def z_end():
-        for s in range(2):
-            arrived(hgf.at[rows_z(far, s * (piece // 2), piece // 2)], zg.at[s, far - 1])
+                own = hgf.at[rows_z(h, -way * i, s * part_z, part_z)]
+            copy(own, own, zg_send, zg.at[h, s, i], (c, at_z(way))).start()
+
+    def z_end(h):
+        for s in range(2):
+            arrived(hgf.at[rows_z(h, far, s * part_z, part_z)], zg.at[h, s, far - 1])
 
     fh, fq = width // 2, width // 4
 
@@ -320,40 +331,50 @@
 
     def g_last():
         arrived(gz.at[pl.ds(0, depth - 1)], g_sem.at[3])
-        ggrad_ref[...] = jnp.sum(gz[...], axis=0) / gain_ref[...]
-
-    z_first()
+        ggrad_ref[...] = (jnp.sum(gz[...], axis=0) / gain).reshape(width)
+
+    for h in range(ZC):
+        z_first(h)
     for du in (2, 1, 3, 0):
         for t in range(2):
             v_first(t, du)
+    z_next(0, 0)
     g_first()
-    z_next(0)
+    z_next(1, 0)
     for t in range(2):
         v_next(t, 2)
-    z_next(1)
-    for du in (1, 3):
-        for t in range(2):
-            v_next(t, du)
-    z_next(2)
+    z_next(0, 1)
+    for t in range(2):
+        v_next(t, 1)
+    z_next(1, 1)
+    for t in range(2):
+        v_next(t, 3)
+    z_next(0, 2)
     for t in range(2):
         v_next(t, 0)
+    z_next(1, 2)
     for t in range(2):
         v_last(t, 2)
         u_first(t)
-    z_last()
-    for du in (1, 3):
-        for t in range(2):
-            v_last(t, du)
+    z_last(0)
+    for t in range(2):
+        v_last(t, 1)
+    z_last(1)
+    for t in range(2):
+        v_last(t, 3)
+    z_spread(0, 1)
     for t in range(2):
         u_next(t)
-    z_spread(1)
+    z_spread(1, 1)
     g_next()
     for t in range(2):
         v_last(t, 0)
-    z_spread(2)
+    z_spread(0, 2)
+    z_spread(1, 2)
     for t in range(2):
         u_last(t)
-    z_spread(3)
+    z_spread(0, 3)
+    z_spread(1, 3)
 
     emb_grad = egrad[...].T
     values = hid_ref[...].astype(F32)
@@ -361,13 +382,14 @@
     spread = jnp.mean(jnp.square(values - center), axis=1, keepdims=True)
     inverse = lax.rsqrt(spread + norm_eps)
     normed = (values - center) * inverse
-    scaled = emb_grad * gain_ref[...]
+    scaled = emb_grad * gain
     first_mean = jnp.mean(scaled, axis=1, keepdims=True)
     second_mean = jnp.mean(scaled * normed, axis=1, keepdims=True)
     igrad_ref[...] = ((scaled - first_mean - normed * second_mean) * inverse).astype(BF16)
 
     g_last()
-    z_end()
+    for h in range(ZC):
+        z_end(h)
     hg_ref[...] = hgf[...]
 
     sent(emb.at[pl.ds(0, PLANE - 1)], ag_send)
@@ -399,7 +421,6 @@
     rows, width = hidden_states.shape
     labels = head_rows.shape[1]
     depth = lax.axis_size("dp")
-    ids = jnp.concatenate([beam_ids.T, positive_ids.T], axis=0).astype(jnp.int16)
     vmem = pl.BlockSpec(memory_space=pltpu.VMEM)
     smem = pl.BlockSpec(memory_space=pltpu.SMEM)
     fh, fq, piece, far = width // 2, width // 4, labels // depth, depth // 2
@@ -409,9 +430,9 @@
         out_shape=(
             jax.ShapeDtypeStruct((labels, width), BF16),
             jax.ShapeDtypeStruct((rows, width), BF16),
-            jax.ShapeDtypeStruct((1, width), F32),
+            jax.ShapeDtypeStruct((width,), F32),
         ),
-        in_specs=[vmem, vmem, vmem, smem, vmem],
+        in_specs=[vmem, vmem, vmem, vmem, smem, vmem],
         out_specs=(vmem, vmem, vmem),
         scratch_shapes=[
             pltpu.VMEM((PLANE, rows, width), BF16),
@@ -427,8 +448,8 @@
             pltpu.VMEM((2, 2, fq, rows), BF16),
             pltpu.VMEM((labels, width), BF16),
             pltpu.VMEM((labels, width), BF16),
-            pltpu.VMEM((2, piece // 2, width), BF16),
-            pltpu.VMEM((2, far - 1, piece, width), BF16),
+            pltpu.VMEM((ZC, 2, piece // ZC // 2, width), BF16),
+            pltpu.VMEM((ZC, 2, far - 1, piece // ZC, width), BF16),
             pltpu.VMEM((PLANE, 1, width), F32),
             pltpu.VMEM((depth, 1, width), F32),
             pltpu.VMEM((width, rows), F32),
@@ -443,20 +464,20 @@
             dma((2, 2)),
             dma((2, 2)),
             dma,
-            dma((2,)),
-            dma((2, far - 1)),
+            dma((ZC, 2)),
+            dma((ZC, 2, far - 1)),
             dma,
-            dma((2, far)),
+            dma((ZC, 2, far)),
             dma((4,)),
         ],
         compiler_params=pltpu.CompilerParams(
-            collective_id=0, has_side_effects=True, vmem_limit_bytes=56 * 1024 * 1024
+            collective_id=0, has_side_effects=True, vmem_limit_bytes=34 * 1024 * 1024
         ),
-    )(hidden_states, ln_gain[None, :], ids, cluster_sizes, head_rows[0])
+    )(hidden_states, ln_gain, beam_ids.T, positive_ids.T, cluster_sizes, head_rows[0])
     new_head, new_first, new_second = adam_update(
         head_rows[0], first_moment[0], second_moment[0], head_grad.astype(F32)
     )
-    return (new_head[None], new_first[None], new_second[None], input_grad, gain_grad[0])
+    return (new_head[None], new_first[None], new_second[None], input_grad, gain_grad)
 
 
 def solution(mesh):

time: 101 us -> 92.2 us (0.913)
  Pallas kernels: 90.6 us -> 79.9 us
  local copies, waits for them, and re-layouts: 1.96 us -> 5.66 us
  other arithmetic: 7.42 us -> 4.66 us
    pallas_call x1, Pallas kernels: 90.6 us -> 79.9 us  [shards(): pl.pallas_call(kernel, out_shape=(jax.ShapeDtypeStruct((labels, width), B...]
    unnamed x7 -> x14, local copies, waits for them, and re-layouts: 0.69 us -> 5.66 us
    broadcast_in_dim x1 -> x0, local copies, waits for them, and re-layouts: 1.27 us -> none  [shards(): ln_gain[None, :]]
where the time goes in v2:
time: 92.2 us; the launch traced here: 91.5 us
  Pallas kernels  79.9 us (87%)
  local copies, waits for them, and re-layouts  5.66 us (6%)
  other arithmetic  4.66 us (5%)
  between operations  1.31 us (1%)
    pallas_call x1, Pallas kernels, shards(): pl.pallas_call(kernel, out_shape=(jax.ShapeDtypeStruct((labels, width), B...  79.9 us
    unnamed x14, local copies, waits for them, and re-layouts  5.66 us
    broadcast_in_dim x1, other arithmetic, shards(): new_second[None]  4.66 us

profile of v2, /device:TPU:2, one launch (start us, length us, event | category | flops | bytes accessed | tf_op | source)
XLA Modules:
  0.0 91.5 jit_solution(9068334912417813733)
XLA Ops:
  1.3 0.0 copy-start
  1.3 1.4 %copy-done = f32[1,512,768]{2,1,0:T(8,128)S(1)} copy-done((f32[1,512,768]{2,1,0:T(8,128)S(1)}, f32[1,512,768]{2,1,0:T(8,128)}, u32[]{:S(2)}) %copy-start) | copy-done | bytes 1572888
  2.7 0.0 copy-start.1
  2.7 0.9 %copy-done.1 = bf16[128,768]{1,0:T(8,128)(2,1)S(1)} copy-done((bf16[128,768]{1,0:T(8,128)(2,1)S(1)}, bf16[128,768]{1,0:T(8,128)(2,1)}, u32[]{:S(2)}) %copy-start.1) | copy-done | bytes 196632
  3.6 0.0 copy-start.2
  3.6 0.7 copy-done.2
  4.3 0.0 copy-start.3
  4.3 0.7 copy-done.3
  5.0 0.0 copy-start.4
  5.0 0.7 copy-done.4
  5.7 0.0 copy-start.5
  5.7 79.9 %shard_map.119 = (bf16[512,768]{1,0:T(8,128)(2,1)S(1)}, bf16[128,768]{1,0:T(8,128)(2,1)S(1)}, f32[768]{0:T(1024)S(1)}) custom-call(bf16[128,768]{1,0:T(8,128)(2,1)S(1)} %copy-done.1, f32[768]{0:T(1024)S(1)} %copy-done.2, s32[8,128]{1,0:T(8,128)S(1)} %bitcast.23, s32[8,128]{1,0:T(8,128)S(1)} %bitcast.24, s32[1]{0:T(128)S(6)} %copy.15.size_ref, ...), custom_call_target="tpu_custom_call" | custom-call | tf_op jit(solution)/shard_map/pallas_call | solution.py:428
  85.6 0.0 copy-done.5
  85.6 4.7 %fusion.3 = (f32[1,512,768]{2,1,0:T(8,128)}, f32[1,512,768]{2,1,0:T(8,128)}, f32[1,512,768]{2,1,0:T(8,128)}) fusion(bf16[512,768]{1,0:T(8,128)(2,1)S(1)} %get-tuple-element.8, f32[1,512,768]{2,1,0:T(8,128)S(1)} %copy-done.5, f32[1,512,768]{2,1,0:T(8,128)} %param.14, f32[1,512,768]{2,1,0:T(8,128)S(1)} %copy-done), kind=kLoop, calls=%fused_computation.6 | loop fusion | flops 5111808 | bytes 10223616 | tf_op jit(solution)/shard_map/broadcast_in_dim | solution.py:480
  90.3 0.7 copy.16
  90.9 0.6 copy.17
Async XLA Ops:
  1.3 1.4 %copy-start = (f32[1,512,768]{2,1,0:T(8,128)S(1)}, f32[1,512,768]{2,1,0:T(8,128)}, u32[]{:S(2)}) copy-start(f32[1,512,768]{2,1,0:T(8,128)} %param.13) | copy-start | bytes 4718596
  2.7 0.9 %copy-start.1 = (bf16[128,768]{1,0:T(8,128)(2,1)S(1)}, bf16[128,768]{1,0:T(8,128)(2,1)}, u32[]{:S(2)}) copy-start(bf16[128,768]{1,0:T(8,128)(2,1)} %hid_ref.1) | copy-start | bytes 589828
  3.6 0.7 copy-start.2
  4.3 0.7 copy-start.3
  5.0 0.7 copy-start.4
  5.7 79.9 %copy-start.5 = (f32[1,512,768]{2,1,0:T(8,128)S(1)}, f32[1,512,768]{2,1,0:T(8,128)}, u32[]{:S(2)}) copy-start(f32[1,512,768]{2,1,0:T(8,128)} %param.15) | copy-start | bytes 4718596

commit v3 on v2

v3 whole, which is shorter than its diff:
```python
import functools

import jax
import jax.numpy as jnp
from jax import lax
from jax.experimental import pallas as pl
from jax.experimental.pallas import tpu as pltpu
from jax.sharding import PartitionSpec as P

MESH = pl.DeviceIdType.MESH
F32 = jnp.float32
BF16 = jnp.bfloat16

norm_eps = 1e-05
learn_rate = 0.01
first_decay = 0.9
second_decay = 0.999
adam_eps = 1e-08
second_fix = 0.632304575226

SIDE = 4
PLANE = 32
CHIPS = (
    (0, 0), (1, 0), (0, 1), (3, 0), (0, 3), (2, 0), (0, 2), (1, 1),
    (3, 3), (1, 3), (3, 1), (2, 1), (1, 2), (2, 3), (3, 2), (2, 2),
)
PLACE = {offset: i for i, offset in enumerate(CHIPS)}
GROUP = 4
ZC = 3


def table_at(values, at):
    half = len(values) // 2
    low = sum(v * 4**i for i, v in enumerate(values[:half]))
    high = sum(v * 4**i for i, v in enumerate(values[half:]))
    above = at // half
    word = low + above * (high - low)
    return lax.rem(lax.shift_right_logical(word, 2 * lax.rem(at, half)), 4)


def kernel(
    size_in, hid_in, gain_in, beam_in, pos_in, head_in, first_in, second_in,
    nh_ref, nf_ref, ns_ref, igrad_ref, ggrad_ref,
    hid, gain_v, beam_v, pos_v, head, first, second,
    emb, ids, wh, wt, hg, slope_v, part, from_core, half_in, quart_in, half_in2, quart_in2,
    hgb, hgf, zq, zh, gc, gx, gy, gz, egrad, normed_v, inverse_v,
    in_sem, ids_send, ids_recv, ag_send, ag_recv, core_recv,
    core_send, rs_core, rs_send, rs_h, rs_q, rs_h2, rs_q2,
    z_send, z_q, z_h, zg_send, zg, g_send, g_recv,
):
    c = lax.axis_index("cluster")
    z = lax.axis_index("dp")
    depth = lax.axis_size("dp")
    rows, width = hid.shape
    labels = head.shape[0]
    beam = beam_v.shape[0]
    x, y, k = c // (2 * SIDE), lax.rem(c // 2, SIDE), lax.rem(c, 2)
    sibling = (c + 1 - 2 * k, z)

    def dev(dx, dy):
        return ((lax.rem(x + dx, SIDE) * SIDE + lax.rem(y + dy, SIDE)) * 2 + k, z)

    def turned(t, du, dv):
        du, dv = du % SIDE, dv % SIDE
        return (du, dv) if t == 0 else (dv, du)

    def copy(src, dst, send, recv, device):
        return pltpu.make_async_remote_copy(
            src_ref=src, dst_ref=dst, send_sem=send, recv_sem=recv, device_id=device, device_id_type=MESH
        )

    def arrived(dst, recv):
        copy(dst, dst, recv, recv, sibling).wait_recv()

    def sent(src, send):
        copy(src, src, send, send, sibling).wait_send()

    loads = [
        pltpu.make_async_copy(src, dst, in_sem.at[i])
        for i, (src, dst) in enumerate(
            (
                (beam_in, beam_v), (pos_in, pos_v), (hid_in, hid), (gain_in, gain_v),
                (head_in, head), (first_in, first), (second_in, second),
            )
        )
    ]
    for load in loads:
        load.start()

    barrier = pltpu.get_barrier_semaphore()
    pl.semaphore_signal(barrier, inc=1, device_id=sibling, device_id_type=MESH)
    for i in range(1, SIDE):
        pl.semaphore_signal(barrier, inc=1, device_id=dev(i, 0), device_id_type=MESH)
        pl.semaphore_signal(barrier, inc=1, device_id=dev(0, i), device_id_type=MESH)

    def greet(i, _):
        pl.semaphore_signal(barrier, inc=1, device_id=(c, lax.rem(z + i, depth)), device_id_type=MESH)
        return _

    lax.fori_loop(1, depth, greet, 0)

    half, quart = rows // 2, rows // 4

    def push(t, at, lo, n, tu, tv):
        du, dv = turned(t, *CHIPS[at])
        to = PLACE[turned(t, du - tu, dv - tv)]
        src, dst = emb.at[2 * at + k, pl.ds(lo, n)], emb.at[2 * to + k, pl.ds(lo, n)]
        copy(src, dst, ag_send, ag_recv.at[t, to], dev(*turned(t, tu, tv))).start()

    def event(at):
        for t in range(2):
            du, dv = turned(t, *CHIPS[at])
            lo = t * half
            if at > 0:
                arrived(emb.at[2 * at + k, pl.ds(lo, half)], ag_recv.at[t, at])
            if dv == 0:
                if du == 0:
                    push(t, at, lo, half, 1, 0)
                    push(t, at, lo, half, -1, 0)
                elif du == 3:
                    push(t, at, lo, quart, 1, 0)
                elif du == 1:
                    push(t, at, lo + quart, quart, -1, 0)
                push(t, at, lo, half, 0, 1)
                push(t, at, lo, half, 0, -1)
            elif dv == 3:
                push(t, at, lo, quart, 0, 1)
            elif dv == 1:
                push(t, at, lo + quart, quart, 0, -1)
        mine = emb.at[2 * at + k]
        copy(mine, mine, ag_send, core_recv.at[at], sibling).start()

    for load in loads[:4]:
        load.wait()
    gain = jnp.concatenate([gain_v[i : i + 1, :] for i in range(width // 128)], axis=1)
    values = hid[...].astype(F32)
    center = jnp.mean(values, axis=1, keepdims=True)
    spread = jnp.mean(jnp.square(values - center), axis=1, keepdims=True)
    inverse = lax.rsqrt(spread + norm_eps)
    normed = (values - center) * inverse
    normed_v[...] = normed
    inverse_v[...] = inverse
    emb[k] = (normed * gain).astype(BF16)
    ids[x, y, k] = jnp.concatenate([beam_v[...], pos_v[...]], axis=0).astype(jnp.int16)
    pl.semaphore_wait(barrier, 1 + 2 * (SIDE - 1) + depth - 1)

    event(0)
    for i in range(1, SIDE):
        own = ids.at[x, y, k]
        copy(own, own, ids_send.at[0], ids_recv.at[0], dev(i, 0)).start()

    loads[4].wait()
    wh[...] = (head[...].astype(BF16) * 0.5).astype(BF16)
    for i in range(width // 128):
        cols = pl.ds(i * 128, 128)
        wt[cols, :] = head[:, cols].T.astype(BF16)
    hg[...] = jnp.zeros_like(hg)
    size = size_in[0]

    arrived(ids.at[pl.ds(0, SIDE - 1), y, k], ids_recv.at[0])
    for i in range(1, SIDE):
        own = ids.at[:, y, k]
        copy(own, own, ids_send.at[1], ids_recv.at[1], dev(0, i)).start()
    event(1)
    event(2)
    arrived(ids.at[:, pl.ds(0, SIDE - 1), k], ids_recv.at[1])
    own = ids.at[:, :, k]
    copy(own, own, ids_send.at[2], ids_recv.at[2], sibling).start()

    many = 2 * GROUP * rows

    def block_of(g):
        return emb[pl.ds(2 * GROUP * g, 2 * GROUP)].reshape(many, width)

    def score(g):
        label, limit = [], []
        for q in range(GROUP):
            at = GROUP * g + q
            arrived(emb.at[2 * at + 1 - k], core_recv.at[at])
            dx, dy = table_at([p[0] for p in CHIPS], at), table_at([p[1] for p in CHIPS], at)
            for s in range(2):
                own = ids[lax.rem(x + dx, SIDE), lax.rem(y + dy, SIDE), s].astype(jnp.int32)
                match = own[0:beam] == c
                place = lax.broadcasted_iota(jnp.int32, (beam, rows), 0)
                place = jnp.sum(jnp.where(match, place, 0), axis=0, keepdims=True)
                chosen = jnp.max(jnp.where(match, 1, 0), axis=0, keepdims=True)
                label.append(own[beam:] - place * labels)
                limit.append(chosen * size)
        label = jnp.concatenate(label, axis=1)
        limit = jnp.concatenate(limit, axis=1)
        logits = lax.dot_general(wh[...], block_of(g), (((1,), (1,)), ((), ())), preferred_element_type=F32)
        word = lax.shift_right_arithmetic(label, 5)
        bit = lax.shift_left(jnp.ones_like(label), label & 31)
        words = lax.broadcasted_iota(jnp.int32, (labels // 32, many), 0)
        bits = jnp.zeros_like(words)
        for p in range(label.shape[0]):
            bits = bits | jnp.where(word[p : p + 1] == words, bit[p : p + 1], 0)
        step = 0.5 / beam
        for i in range(labels // 32):
            slot = lax.broadcasted_iota(jnp.int32, (32, many), 0)
            hit = lax.shift_left(jnp.broadcast_to(bits[i : i + 1], (32, many)), 31 - slot) < 0
            slope = step * jnp.tanh(logits[32 * i : 32 * i + 32]) + jnp.where(hit, -step, step)
            slope = jnp.where(slot + 32 * i < limit, slope, 0.0)
            slope_v[pl.ds(32 * i, 32), :] = slope.astype(BF16)

    def gather_head(g):
        hg[...] += jnp.dot(slope_v[...], block_of(g), preferred_element_type=F32)

    def back(g):
        grads = jnp.dot(wt[...], slope_v[...], preferred_element_type=F32).astype(BF16)
        for q in range(GROUP):
            for s in range(2):
                i = 2 * q + s
                part[GROUP * g + q, s] = grads[:, i * rows : (i + 1) * rows]
        there = pl.ds(GROUP * g, GROUP)
        copy(part.at[there, 1 - k], from_core.at[there], core_send, rs_core.at[g], sibling).start()

    def join(g):
        arrived(from_core.at[pl.ds(GROUP * g, GROUP)], rs_core.at[g])
        for q in range(GROUP):
            part[GROUP * g + q, k] += from_core[GROUP * g + q]

    groups = len(CHIPS) // GROUP

    def turn(g, _):
        def events(shift):
            for i in range(groups):
                if GROUP * i + shift < len(CHIPS):
                    pl.when(g == i)(functools.partial(event, GROUP * i + shift))

        events(3)

        @pl.when(g == 0)
        def _ids():
            arrived(ids.at[:, :, k], ids_recv.at[2])

        @pl.when(g >= 1)
        def _back():
            back(g - 1)

        events(4)
        score(g)
        events(5)

        @pl.when(g >= 2)
        def _join():
            join(g - 2)

        gather_head(g)
        events(6)
        return _

    lax.fori_loop(0, groups, turn, 0)

    piece = labels // depth
    part_z = piece // 2
    far = depth // 2
    wide = width // ZC

    def at_z(i):
        return lax.rem(z + i + depth, depth)

    def rows_z(i, lo=0, n=piece):
        return pl.ds(pl.multiple_of(at_z(i) * piece + lo, part_z), n)

    def z_first(h):
        hgb[h] = hg[:, h * wide : (h + 1) * wide].astype(BF16)
        for s in range(2):
            src = hgb.at[h, rows_z(far, s * part_z, part_z)]
            copy(src, zq.at[h, s], z_send, z_q.at[h, s], (c, at_z(1 - 2 * s))).start()

    def z_next(h, i):
        for s in range(2):
            way = 1 - 2 * s
            own = rows_z(way * (far - 1 - i))
            if i == 0:
                arrived(zq.at[h, s], z_q.at[h, s])
                mid = rows_z(way * (far - 1), s * part_z, part_z)
                hgb[h, mid] += zq[h, s]
            else:
                arrived(zh.at[h, s, i - 1], z_h.at[h, s, i - 1])
                hgb[h, own] += zh[h, s, i - 1]
            copy(hgb.at[h, own], zh.at[h, s, i], z_send, z_h.at[h, s, i], (c, at_z(way))).start()

    def adam(h, at):
        cols = pl.ds(h * wide, wide)
        grad = hgf[h, at].astype(F32)
        new_first = first_decay * first[at, cols] + (1.0 - first_decay) * grad
        new_second = second_decay * second[at, cols] + (1.0 - second_decay) * grad * grad
        nf_ref[at, cols] = new_first
        ns_ref[at, cols] = new_second
        step_size = new_first / (jnp.sqrt(new_second * (1.0 / second_fix)) + adam_eps)
        nh_ref[at, cols] = head[at, cols] - learn_rate * step_size

    def z_last(h):
        total = hgb[h, rows_z(0)].astype(F32)
        for s in range(2):
            arrived(zh.at[h, s, far - 2], z_h.at[h, s, far - 2])
            total += zh[h, s, far - 2].astype(F32)
        hgf[h, rows_z(0)] = total.astype(BF16)
        for s in range(2):
            own = hgf.at[h, rows_z(0)]
            copy(own, own, zg_send, zg.at[h, s, 0], (c, at_z(1 - 2 * s))).start()

    def z_spread(h, i):
        for s in range(2):
            way = 1 - 2 * s
            own = hgf.at[h, rows_z(-way * i)]
            arrived(own, zg.at[h, s, i - 1])
            if i == far - 1:
                own = hgf.at[h, rows_z(-way * i, s * part_z, part_z)]
            copy(own, own, zg_send, zg.at[h, s, i], (c, at_z(way))).start()

    def z_adam(h, i):
        adam(h, rows_z(i))
        adam(h, rows_z(-i))

    def z_end(h):
        for s in range(2):
            arrived(hgf.at[h, rows_z(far, s * part_z, part_z)], zg.at[h, s, far - 1])
        adam(h, rows_z(far))

    fh, fq = width // 2, width // 4

    def feats(t, lo, n):
        return pl.ds(t * fh + lo, n)

    def dest(t, du, dv):
        return PLACE[turned(t, du, dv)]

    def v_first(t, du):
        for s in range(2):
            src = part.at[dest(t, du, 2), k, feats(t, s * fq, fq)]
            to = dev(*turned(t, 0, 1 - 2 * s))
            copy(src, quart_in.at[t, du, s], rs_send, rs_q.at[t, du, s], to).start()

    def v_next(t, du):
        for s in range(2):
            arrived(quart_in.at[t, du, s], rs_q.at[t, du, s])
            to = dest(t, du, 1 - 2 * s)
            part[to, k, feats(t, s * fq, fq)] += quart_in[t, du, s]
            src = part.at[to, k, feats(t, 0, fh)]
            copy(src, half_in.at[t, du, s], rs_send, rs_h.at[t, du, s], dev(*turned(t, 0, 1 - 2 * s))).start()

    def v_last(t, du):
        to = dest(t, du, 0)
        for s in range(2):
            arrived(half_in.at[t, du, s], rs_h.at[t, du, s])
        total = part[to, k, feats(t, 0, fh)].astype(F32)
        total += half_in[t, du, 0].astype(F32) + half_in[t, du, 1].astype(F32)
        part[to, k, feats(t, 0, fh)] = total.astype(BF16)

    def u_first(t):
        for s in range(2):
            src = part.at[dest(t, 2, 0), k, feats(t, s * fq, fq)]
            copy(src, quart_in2.at[t, s], rs_send, rs_q2.at[t, s], dev(*turned(t, 1 - 2 * s, 0))).start()

    def u_next(t):
        for s in range(2):
            arrived(quart_in2.at[t, s], rs_q2.at[t, s])
            to = dest(t, 1 - 2 * s, 0)
            part[to, k, feats(t, s * fq, fq)] += quart_in2[t, s]
            src = part.at[to, k, feats(t, 0, fh)]
            copy(src, half_in2.at[t, s], rs_send, rs_h2.at[t, s], dev(*turned(t, 1 - 2 * s, 0))).start()

    def u_last(t):
        for s in range(2):
            arrived(half_in2.at[t, s], rs_h2.at[t, s])
        total = part[0, k, feats(t, 0, fh)].astype(F32)
        total += half_in2[t, 0].astype(F32) + half_in2[t, 1].astype(F32)
        egrad[:, t * fh : (t + 1) * fh] = total.T

    def g_first():
        gc[k] = jnp.sum(wh[...].astype(F32) * hg[...], axis=0, keepdims=True) * 2.0
        copy(gc.at[k], gc.at[k], g_send.at[0], g_recv.at[0], sibling).start()

    def g_x():
        arrived(gc.at[0], g_recv.at[0])
        gx[x] = gc[0] + gc[1]
        for i in range(1, SIDE):
            copy(gx.at[x], gx.at[x], g_send.at[1], g_recv.at[1], dev(i, 0)).start()

    def g_y():
        arrived(gx.at[pl.ds(0, SIDE - 1)], g_recv.at[1])
        gy[y] = jnp.sum(gx[...], axis=0)
        for i in range(1, SIDE):
            copy(gy.at[y], gy.at[y], g_send.at[2], g_recv.at[2], dev(0, i)).start()

    def g_z():
        arrived(gy.at[pl.ds(0, SIDE - 1)], g_recv.at[2])
        gz[z] = jnp.sum(gy[...], axis=0)

        def send(i, _):
            copy(gz.at[z], gz.at[z], g_send.at[3], g_recv.at[3], (c, at_z(i))).start()
            return _

        lax.fori_loop(1, depth, send, 0)

    def g_last():
        arrived(gz.at[pl.ds(0, depth - 1)], g_recv.at[3])
        total = jnp.sum(gz[...], axis=0) / gain
        for i in range(width // 128):
            ggrad_ref[i : i + 1, :] = total[:, i * 128 : (i + 1) * 128]

    chunks = range(ZC)
    for h in chunks:
        z_first(h)
    back(groups - 1)
    join(groups - 2)
    g_first()
    for h in chunks:
        z_next(h, 0)
    join(groups - 1)
    for du in (2, 1, 3, 0):
        for t in range(2):
            v_first(t, du)
    g_x()
    for h in chunks:
        z_next(h, 1)
    for t in range(2):
        v_next(t, 2)
    for t in range(2):
        v_next(t, 1)
    z_next(0, 2)
    for t in range(2):
        v_next(t, 3)
    z_next(1, 2)
    z_next(2, 2)
    for t in range(2):
        v_next(t, 0)
    g_y()
    z_last(0)
    for t in range(2):
        v_last(t, 2)
        u_first(t)
    z_last(1)
    z_last(2)
    loads[5].wait()
    loads[6].wait()
    for t in range(2):
        v_last(t, 1)
    for h in chunks:
        z_spread(h, 1)
    g_z()
    for t in range(2):
        v_last(t, 3)
    for t in range(2):
        u_next(t)
    for h in chunks:
        z_spread(h, 2)
        adam(h, rows_z(0))
    for t in range(2):
        v_last(t, 0)
    for h in chunks:
        z_adam(h, 1)
    for h in chunks:
        z_spread(h, 3)
    for t in range(2):
        u_last(t)
    for h in chunks:
        z_adam(h, 2)

    scaled = egrad[...] * gain
    normed = normed_v[...]
    first_mean = jnp.mean(scaled, axis=1, keepdims=True)
    second_mean = jnp.mean(scaled * normed, axis=1, keepdims=True)
    igrad_ref[...] = ((scaled - first_mean - normed * second_mean) * inverse_v[...]).astype(BF16)

    for h in chunks:
        z_adam(h, 3)
    g_last()
    for h in chunks:
        z_end(h)

    sent(emb.at[pl.ds(0, PLANE - 1)], ag_send)
    sent(from_core, core_send)
    sent(from_core.at[pl.ds(0, PLANE // 2 - 1)], rs_send)
    sent(ids.at[pl.ds(0, SIDE - 1), y, k], ids_send.at[0])
    sent(ids.at[:, pl.ds(0, SIDE - 1), k], ids_send.at[1])
    sent(ids.at[:, :, k], ids_send.at[2])
    sent(gc.at[0], g_send.at[0])
    sent(gx.at[pl.ds(0, SIDE - 1)], g_send.at[1])
    sent(gy.at[pl.ds(0, SIDE - 1)], g_send.at[2])
    sent(gz.at[pl.ds(0, depth - 1)], g_send.at[3])
    sent(hgb.at[:, pl.ds(0, labels - piece)], z_send)
    sent(hgf.at[:, pl.ds(0, labels - piece)], zg_send)


def store(nh, nf, ns, igrad, ggrad, nh_out, nf_out, ns_out, igrad_out, ggrad_out, sem):
    pairs = ((nh, nh_out.at[0]), (nf, nf_out.at[0]), (ns, ns_out.at[0]), (igrad, igrad_out), (ggrad, ggrad_out))
    copies = [pltpu.make_async_copy(src, dst, sem.at[i]) for i, (src, dst) in enumerate(pairs)]
    for copy in copies:
        copy.start()
    for copy in copies:
        copy.wait()


def shards(
    hidden_states,
    ln_gain,
    beam_ids,
    positive_ids,
    cluster_sizes,
    head_rows,
    first_moment,
    second_moment,
):
    rows, width = hidden_states.shape
    labels = head_rows.shape[1]
    beam, pos = beam_ids.shape[1], positive_ids.shape[1]
    depth = lax.axis_size("dp")
    vmem = pl.BlockSpec(memory_space=pltpu.VMEM)
    hbm = pl.BlockSpec(memory_space=pltpu.HBM)
    fh, fq, piece, far, wide = width // 2, width // 4, labels // depth, depth // 2, width // ZC
    dma = pltpu.SemaphoreType.DMA
    head_shape = pltpu.VMEM((labels, width), F32)
    results = pl.pallas_call(
        kernel,
        out_shape=(
            head_shape,
            head_shape,
            head_shape,
            pltpu.VMEM((rows, width), BF16),
            pltpu.VMEM((width // 128, 128), F32),
        ),
        in_specs=[pl.BlockSpec(memory_space=pltpu.SMEM)] + [hbm] * 7,
        out_specs=(vmem,) * 5,
        scratch_shapes=[
            pltpu.VMEM((rows, width), BF16),
            pltpu.VMEM((width // 128, 128), F32),
            pltpu.VMEM((beam, rows), jnp.int32),
            pltpu.VMEM((pos, rows), jnp.int32),
            pltpu.VMEM((labels, width), F32),
            pltpu.VMEM((labels, width), F32),
            pltpu.VMEM((labels, width), F32),
            pltpu.VMEM((PLANE, rows, width), BF16),
            pltpu.VMEM((SIDE, SIDE, 2, beam + pos, rows), jnp.int16),
            pltpu.VMEM((labels, width), BF16),
            pltpu.VMEM((width, labels), BF16),
            pltpu.VMEM((labels, width), F32),
            pltpu.VMEM((labels, 2 * GROUP * rows), BF16),
            pltpu.VMEM((PLANE // 2, 2, width, rows), BF16),
            pltpu.VMEM((PLANE // 2, width, rows), BF16),
            pltpu.VMEM((2, SIDE, 2, fh, rows), BF16),
            pltpu.VMEM((2, SIDE, 2, fq, rows), BF16),
            pltpu.VMEM((2, 2, fh, rows), BF16),
            pltpu.VMEM((2, 2, fq, rows), BF16),
            pltpu.VMEM((ZC, labels, wide), BF16),
            pltpu.VMEM((ZC, labels, wide), BF16),
            pltpu.VMEM((ZC, 2, piece // 2, wide), BF16),
            pltpu.VMEM((ZC, 2, far - 1, piece, wide), BF16),
            pltpu.VMEM((2, 1, width), F32),
            pltpu.VMEM((SIDE, 1, width), F32),
            pltpu.VMEM((SIDE, 1, width), F32),
            pltpu.VMEM((depth, 1, width), F32),
            pltpu.VMEM((rows, width), F32),
            pltpu.VMEM((rows, width), F32),
            pltpu.VMEM((rows, 1), F32),
            dma((7,)),
            dma((3,)),
            dma((3,)),
            dma,
            dma((2, len(CHIPS))),
            dma((len(CHIPS),)),
            dma,
            dma((len(CHIPS) // GROUP,)),
            dma,
            dma((2, SIDE, 2)),
            dma((2, SIDE, 2)),
            dma((2, 2)),
            dma((2, 2)),
            dma,
            dma((ZC, 2)),
            dma((ZC, 2, far - 1)),
            dma,
            dma((ZC, 2, far)),
            dma((4,)),
            dma((4,)),
        ],
        compiler_params=pltpu.CompilerParams(
            collective_id=0, has_side_effects=True, vmem_limit_bytes=48 * 1024 * 1024
        ),
    )(
        cluster_sizes,
        *(
            pltpu.with_memory_space_constraint(a, pltpu.HBM)
            for a in (
                hidden_states, ln_gain.reshape(width // 128, 128), beam_ids.T, positive_ids.T,
                head_rows[0], first_moment[0], second_moment[0],
            )
        ),
    )
    whole = pltpu.HBM((1, labels, width), F32)
    *rest, gain_grad = pl.pallas_call(
        store,
        out_shape=(whole, whole, whole, *[pltpu.HBM(r.shape, r.dtype) for r in results[3:]]),
        in_specs=[pl.BlockSpec(memory_space=pl.ANY)] * 5,
        out_specs=(hbm,) * 5,
        scratch_shapes=[dma((5,))],
        compiler_params=pltpu.CompilerParams(vmem_limit_bytes=16 * 1024 * 1024),
    )(*(pltpu.with_memory_space_constraint(r, pltpu.VMEM) for r in results))
    return (*rest, gain_grad.reshape(width))


def solution(mesh):
    in_specs = (
        P(("cluster", "dp"), None),
        P(),
        P(("cluster", "dp"), None),
        P(("cluster", "dp"), None),
        P("cluster"),
        P("cluster", None, None),
        P("cluster", None, None),
        P("cluster", None, None),
    )
    out_specs = (
        P("cluster", None, None),
        P("cluster", None, None),
        P("cluster", None, None),
        P(("cluster", "dp"), None),
        P(),
    )
    return jax.shard_map(shards, mesh=mesh, in_specs=in_specs, out_specs=out_specs, check_vma=False)
```

time: 92.2 us -> 77.7 us (0.84)
  local copies, waits for them, and re-layouts: 5.66 us -> 0 us
  other arithmetic: 4.66 us -> 0 us
  Pallas kernels: 79.9 us -> 76.4 us
    unnamed x14 -> x0, local copies, waits for them, and re-layouts: 5.66 us -> none
    broadcast_in_dim x1 -> x0, other arithmetic: 4.66 us -> none  [shards(): new_second[None]]
    pallas_call x1 -> x2, Pallas kernels: 79.9 us -> 76.4 us  [the longest x1 74.1 us: shards(): pl.pallas_call(kernel, out_shape=(head_shape, head_shape, head_shape, plt...]
where the time goes in v3:
time: 77.7 us; the launch traced here: 77.6 us
  Pallas kernels  76.4 us (98%)
  between operations  1.29 us (2%)
    pallas_call x1, Pallas kernels, shards(): pl.pallas_call(kernel, out_shape=(head_shape, head_shape, head_shape, plt...  74.1 us
    pallas_call x1, Pallas kernels, shards(): pl.pallas_call(store, out_shape=(whole, whole, whole, *[pltpu.HBM(r.shape...  2.28 us

profile of v3, /device:TPU:2, one launch (start us, length us, event | category | flops | bytes accessed | tf_op | source)
XLA Modules:
  0.0 77.6 jit_solution(5174159642603870601)
XLA Ops:
  1.3 74.1 %shard_map.119 = (f32[512,768]{1,0:T(8,128)S(1)}, f32[512,768]{1,0:T(8,128)S(1)}, f32[512,768]{1,0:T(8,128)S(1)}, bf16[128,768]{1,0:T(8,128)(2,1)S(1)}, f32[6,128]{1,0:T(8,128)S(1)}) custom-call(s32[1]{0:T(128)S(6)} %copy.13.size_in, bf16[128,768]{1,0:T(8,128)(2,1)} %hid_in.1, f32[6,128]{1,0:T(8,128)} %bitcast.10, s32[8,128]{1,0:T(8,128)} %bitcast.11, ...), custom_call_target="tpu_custom_call" | custom-call | tf_op jit(solution)/shard_map/pallas_call | solution.py:517
  75.4 2.3 %shard_map.120 = (f32[1,512,768]{2,1,0:T(8,128)}, f32[1,512,768]{2,1,0:T(8,128)}, f32[1,512,768]{2,1,0:T(8,128)}, bf16[128,768]{1,0:T(8,128)(2,1)}, f32[6,128]{1,0:T(8,128)}) custom-call(f32[512,768]{1,0:T(8,128)S(1)} %get-tuple-element.15.nh, f32[512,768]{1,0:T(8,128)S(1)} %get-tuple-element.16.nf, f32[512,768]{1,0:T(8,128)S(1)} %get-tuple-element.17.ns, ...), custom_call_target="tpu_custom_call" | custom-call | tf_op jit(solution)/shard_map/pallas_call | solution.py:594

commit v4 on v3

--- a/solution.py
+++ b/solution.py
@@ -25,17 +25,9 @@
     (3, 3), (1, 3), (3, 1), (2, 1), (1, 2), (2, 3), (3, 2), (2, 2),
 )
 PLACE = {offset: i for i, offset in enumerate(CHIPS)}
-GROUP = 4
+GROUPS = ((0, 5), (5, 3), (8, 3), (11, 5))
+MOST = max(n for _, n in GROUPS)
 ZC = 3
-
-
-def table_at(values, at):
-    half = len(values) // 2
-    low = sum(v * 4**i for i, v in enumerate(values[:half]))
-    high = sum(v * 4**i for i, v in enumerate(values[half:]))
-    above = at // half
-    word = low + above * (high - low)
-    return lax.rem(lax.shift_right_logical(word, 2 * lax.rem(at, half)), 4)
 
 
 def kernel(
@@ -107,28 +99,32 @@
         src, dst = emb.at[2 * at + k, pl.ds(lo, n)], emb.at[2 * to + k, pl.ds(lo, n)]
         copy(src, dst, ag_send, ag_recv.at[t, to], dev(*turned(t, tu, tv))).start()
 
-    def event(at):
-        for t in range(2):
-            du, dv = turned(t, *CHIPS[at])
-            lo = t * half
-            if at > 0:
-                arrived(emb.at[2 * at + k, pl.ds(lo, half)], ag_recv.at[t, at])
-            if dv == 0:
-                if du == 0:
-                    push(t, at, lo, half, 1, 0)
-                    push(t, at, lo, half, -1, 0)
-                elif du == 3:
-                    push(t, at, lo, quart, 1, 0)
-                elif du == 1:
-                    push(t, at, lo + quart, quart, -1, 0)
-                push(t, at, lo, half, 0, 1)
-                push(t, at, lo, half, 0, -1)
-            elif dv == 3:
-                push(t, at, lo, quart, 0, 1)
-            elif dv == 1:
-                push(t, at, lo + quart, quart, 0, -1)
-        mine = emb.at[2 * at + k]
-        copy(mine, mine, ag_send, core_recv.at[at], sibling).start()
+    def half_in_hand(t, du, dv):
+        at, lo = PLACE[turned(t, du, dv)], t * half
+        if at > 0:
+            arrived(emb.at[2 * at + k, pl.ds(lo, half)], ag_recv.at[t, at])
+        if dv == 0:
+            if du == 0:
+                push(t, at, lo, half, 1, 0)
+                push(t, at, lo, half, -1, 0)
+            elif du == 3:
+                push(t, at, lo, quart, 1, 0)
+            elif du == 1:
+                push(t, at, lo + quart, quart, -1, 0)
+            push(t, at, lo, half, 0, 1)
+            push(t, at, lo, half, 0, -1)
+        elif dv == 3:
+            push(t, at, lo, quart, 0, 1)
+        elif dv == 1:
+            push(t, at, lo + quart, quart, 0, -1)
+
+    def event(*offsets, whole=()):
+        for du, dv in offsets:
+            for t in range(2):
+                half_in_hand(t, du, dv)
+        for offset in whole:
+            mine = emb.at[2 * PLACE[offset] + k]
+            copy(mine, mine, ag_send, core_recv.at[PLACE[offset]], sibling).start()
 
     for load in loads[:4]:
         load.wait()
@@ -144,7 +140,7 @@
     ids[x, y, k] = jnp.concatenate([beam_v[...], pos_v[...]], axis=0).astype(jnp.int16)
     pl.semaphore_wait(barrier, 1 + 2 * (SIDE - 1) + depth - 1)
 
-    event(0)
+    event((0, 0), whole=((0, 0),))
     for i in range(1, SIDE):
         own = ids.at[x, y, k]
         copy(own, own, ids_send.at[0], ids_recv.at[0], dev(i, 0)).start()
@@ -161,23 +157,29 @@
     for i in range(1, SIDE):
         own = ids.at[:, y, k]
         copy(own, own, ids_send.at[1], ids_recv.at[1], dev(0, i)).start()
-    event(1)
-    event(2)
+    event((1, 0), (3, 0))
+    event((0, 1), (0, 3), whole=((1, 0), (0, 1), (3, 0), (0, 3)))
     arrived(ids.at[:, pl.ds(0, SIDE - 1), k], ids_recv.at[1])
     own = ids.at[:, :, k]
     copy(own, own, ids_send.at[2], ids_recv.at[2], sibling).start()
 
-    many = 2 * GROUP * rows
+    def chips_of(g):
+        first, n = GROUPS[g]
+        return range(first, first + n)
 
     def block_of(g):
-        return emb[pl.ds(2 * GROUP * g, 2 * GROUP)].reshape(many, width)
+        first, n = GROUPS[g]
+        return emb[pl.ds(2 * first, 2 * n)].reshape(2 * n * rows, width)
+
+    def slope_of(g):
+        return slope_v[:, : 2 * GROUPS[g][1] * rows]
 
     def score(g):
         label, limit = [], []
-        for q in range(GROUP):
-            at = GROUP * g + q
+        many = 2 * GROUPS[g][1] * rows
+        for at in chips_of(g):
             arrived(emb.at[2 * at + 1 - k], core_recv.at[at])
-            dx, dy = table_at([p[0] for p in CHIPS], at), table_at([p[1] for p in CHIPS], at)
+            dx, dy = CHIPS[at]
             for s in range(2):
                 own = ids[lax.rem(x + dx, SIDE), lax.rem(y + dy, SIDE), s].astype(jnp.int32)
                 match = own[0:beam] == c
@@ -201,56 +203,47 @@
             hit = lax.shift_left(jnp.broadcast_to(bits[i : i + 1], (32, many)), 31 - slot) < 0
             slope = step * jnp.tanh(logits[32 * i : 32 * i + 32]) + jnp.where(hit, -step, step)
             slope = jnp.where(slot + 32 * i < limit, slope, 0.0)
-            slope_v[pl.ds(32 * i, 32), :] = slope.astype(BF16)
+            slope_v[pl.ds(32 * i, 32), :many] = slope.astype(BF16)
 
     def gather_head(g):
-        hg[...] += jnp.dot(slope_v[...], block_of(g), preferred_element_type=F32)
+        hg[...] += jnp.dot(slope_of(g), block_of(g), preferred_element_type=F32)
 
     def back(g):
-        grads = jnp.dot(wt[...], slope_v[...], preferred_element_type=F32).astype(BF16)
-        for q in range(GROUP):
+        grads = jnp.dot(wt[...], slope_of(g), preferred_element_type=F32).astype(BF16)
+        for q, at in enumerate(chips_of(g)):
             for s in range(2):
                 i = 2 * q + s
-                part[GROUP * g + q, s] = grads[:, i * rows : (i + 1) * rows]
-        there = pl.ds(GROUP * g, GROUP)
+                part[at, s] = grads[:, i * rows : (i + 1) * rows]
+        there = pl.ds(*GROUPS[g])
         copy(part.at[there, 1 - k], from_core.at[there], core_send, rs_core.at[g], sibling).start()
 
     def join(g):
-        arrived(from_core.at[pl.ds(GROUP * g, GROUP)], rs_core.at[g])
-        for q in range(GROUP):
-            part[GROUP * g + q, k] += from_core[GROUP * g + q]
-
-    groups = len(CHIPS) // GROUP
-
-    def turn(g, _):
-        def events(shift):
-            for i in range(groups):
-                if GROUP * i + shift < len(CHIPS):
-                    pl.when(g == i)(functools.partial(event, GROUP * i + shift))
-
-        events(3)
-
-        @pl.when(g == 0)
-        def _ids():
-            arrived(ids.at[:, :, k], ids_recv.at[2])
-
-        @pl.when(g >= 1)
-        def _back():
-            back(g - 1)
-
-        events(4)
-        score(g)
-        events(5)
-
-        @pl.when(g >= 2)
-        def _join():
-            join(g - 2)
-
-        gather_head(g)
-        events(6)
-        return _
-
-    lax.fori_loop(0, groups, turn, 0)
+        arrived(from_core.at[pl.ds(*GROUPS[g])], rs_core.at[g])
+        for at in chips_of(g):
+            part[at, k] += from_core[at]
+
+    arrived(ids.at[:, :, k], ids_recv.at[2])
+    score(0)
+    gather_head(0)
+    event((2, 0))
+    back(0)
+    event((1, 1), whole=((1, 1),))
+    event((0, 2), whole=((2, 0), (0, 2)))
+    score(1)
+    event((3, 3), whole=((3, 3),))
+    event((1, 3), (3, 1), whole=((1, 3), (3, 1)))
+    gather_head(1)
+    back(1)
+    join(0)
+    score(2)
+    event((2, 1), (2, 3))
+    gather_head(2)
+    back(2)
+    join(1)
+    event((1, 2), (3, 2), whole=((2, 1), (1, 2), (2, 3), (3, 2)))
+    event((2, 2), whole=((2, 2),))
+    score(3)
+    gather_head(3)
 
     piece = labels // depth
     part_z = piece // 2
@@ -405,12 +398,12 @@
     chunks = range(ZC)
     for h in chunks:
         z_first(h)
-    back(groups - 1)
-    join(groups - 2)
+    back(3)
+    join(2)
     g_first()
     for h in chunks:
         z_next(h, 0)
-    join(groups - 1)
+    join(3)
     for du in (2, 1, 3, 0):
         for t in range(2):
             v_first(t, du)
@@ -421,20 +414,22 @@
         v_next(t, 2)
     for t in range(2):
         v_next(t, 1)
-    z_next(0, 2)
+    for h in chunks[: ZC // 2]:
+        z_next(h, 2)
     for t in range(2):
         v_next(t, 3)
-    z_next(1, 2)
-    z_next(2, 2)
+    for h in chunks[ZC // 2 :]:
+        z_next(h, 2)
     for t in range(2):
         v_next(t, 0)
     g_y()
-    z_last(0)
+    for h in chunks[: ZC // 2]:
+        z_last(h)
     for t in range(2):
         v_last(t, 2)
         u_first(t)
-    z_last(1)
-    z_last(2)
+    for h in chunks[ZC // 2 :]:
+        z_last(h)
     loads[5].wait()
     loads[6].wait()
     for t in range(2):
@@ -538,7 +533,7 @@
             pltpu.VMEM((labels, width), BF16),
             pltpu.VMEM((width, labels), BF16),
             pltpu.VMEM((labels, width), F32),
-            pltpu.VMEM((labels, 2 * GROUP * rows), BF16),
+            pltpu.VMEM((labels, 2 * MOST * rows), BF16),
             pltpu.VMEM((PLANE // 2, 2, width, rows), BF16),
             pltpu.VMEM((PLANE // 2, width, rows), BF16),
             pltpu.VMEM((2, SIDE, 2, fh, rows), BF16),
@@ -563,7 +558,7 @@
             dma((2, len(CHIPS))),
             dma((len(CHIPS),)),
             dma,
-            dma((len(CHIPS) // GROUP,)),
+            dma((len(GROUPS),)),
             dma,
             dma((2, SIDE, 2)),
             dma((2, SIDE, 2)),

time: 77.7 us -> 72.8 us (0.937); the launches traced: 77.6 us -> 71.8 us
  Pallas kernels: 76.4 us -> 70.4 us
    pallas_call x1, Pallas kernels: 74.1 us -> 68.1 us  [shards(): pl.pallas_call(kernel, out_shape=(head_shape, head_shape, head_shape, plt...]
where the time goes in v4:
time: 72.8 us; the launch traced here: 71.8 us
  Pallas kernels  70.4 us (97%)
  between operations  1.45 us (2%)
    pallas_call x1, Pallas kernels, shards(): pl.pallas_call(kernel, out_shape=(head_shape, head_shape, head_shape, plt...  68.1 us
    pallas_call x1, Pallas kernels, shards(): pl.pallas_call(store, out_shape=(whole, whole, whole, *[pltpu.HBM(r.shape...  2.28 us

profile of v4, /device:TPU:2, one launch (start us, length us, event | category | flops | bytes accessed | tf_op | source)
XLA Modules:
  0.0 71.8 jit_solution(7087160565088194847)
XLA Ops:
  1.3 68.1 %shard_map.119 = (f32[512,768]{1,0:T(8,128)S(1)}, f32[512,768]{1,0:T(8,128)S(1)}, f32[512,768]{1,0:T(8,128)S(1)}, bf16[128,768]{1,0:T(8,128)(2,1)S(1)}, f32[6,128]{1,0:T(8,128)S(1)}) custom-call(s32[1]{0:T(128)S(6)} %copy.13.size_in, bf16[128,768]{1,0:T(8,128)(2,1)} %hid_in.1, f32[6,128]{1,0:T(8,128)} %bitcast.10, s32[8,128]{1,0:T(8,128)} %bitcast.11, ...), custom_call_target="tpu_custom_call" | custom-call | tf_op jit(solution)/shard_map/pallas_call | solution.py:512
  69.4 2.3 %shard_map.120 = (f32[1,512,768]{2,1,0:T(8,128)}, f32[1,512,768]{2,1,0:T(8,128)}, f32[1,512,768]{2,1,0:T(8,128)}, bf16[128,768]{1,0:T(8,128)(2,1)}, f32[6,128]{1,0:T(8,128)}) custom-call(f32[512,768]{1,0:T(8,128)S(1)} %get-tuple-element.15.nh, f32[512,768]{1,0:T(8,128)S(1)} %get-tuple-element.16.nf, f32[512,768]{1,0:T(8,128)S(1)} %get-tuple-element.17.ns, ...), custom_call_target="tpu_custom_call" | custom-call | tf_op jit(solution)/shard_map/pallas_call | solution.py:589

commit v5 on v4

--- a/solution.py
+++ b/solution.py
@@ -35,7 +35,7 @@
     nh_ref, nf_ref, ns_ref, igrad_ref, ggrad_ref,
     hid, gain_v, beam_v, pos_v, head, first, second,
     emb, ids, wh, wt, hg, slope_v, part, from_core, half_in, quart_in, half_in2, quart_in2,
-    hgb, hgf, zq, zh, gc, gx, gy, gz, egrad, normed_v, inverse_v,
+    hgb, hgf, zq, zh, gp, gc, gz, egrad, normed_v, inverse_v,
     in_sem, ids_send, ids_recv, ag_send, ag_recv, core_recv,
     core_send, rs_core, rs_send, rs_h, rs_q, rs_h2, rs_q2,
     z_send, z_q, z_h, zg_send, zg, g_send, g_recv,
@@ -52,6 +52,9 @@
     def dev(dx, dy):
         return ((lax.rem(x + dx, SIDE) * SIDE + lax.rem(y + dy, SIDE)) * 2 + k, z)
 
+    def chip_peer(i):
+        return (lax.rem(c // 2 + i, SIDE * SIDE) * 2 + k, z)
+
     def turned(t, du, dv):
         du, dv = du % SIDE, dv % SIDE
         return (du, dv) if t == 0 else (dv, du)
@@ -81,14 +84,16 @@
 
     barrier = pltpu.get_barrier_semaphore()
     pl.semaphore_signal(barrier, inc=1, device_id=sibling, device_id_type=MESH)
-    for i in range(1, SIDE):
-        pl.semaphore_signal(barrier, inc=1, device_id=dev(i, 0), device_id_type=MESH)
-        pl.semaphore_signal(barrier, inc=1, device_id=dev(0, i), device_id_type=MESH)
+
+    def greet_plane(i, _):
+        pl.semaphore_signal(barrier, inc=1, device_id=chip_peer(i), device_id_type=MESH)
+        return _
 
     def greet(i, _):
         pl.semaphore_signal(barrier, inc=1, device_id=(c, lax.rem(z + i, depth)), device_id_type=MESH)
         return _
 
+    lax.fori_loop(1, SIDE * SIDE, greet_plane, 0)
     lax.fori_loop(1, depth, greet, 0)
 
     half, quart = rows // 2, rows // 4
@@ -99,20 +104,23 @@
         src, dst = emb.at[2 * at + k, pl.ds(lo, n)], emb.at[2 * to + k, pl.ds(lo, n)]
         copy(src, dst, ag_send, ag_recv.at[t, to], dev(*turned(t, tu, tv))).start()
 
-    def half_in_hand(t, du, dv):
+    def half_in_hand(t, du, dv, early=True, late=True):
         at, lo = PLACE[turned(t, du, dv)], t * half
-        if at > 0:
+        if at > 0 and early:
             arrived(emb.at[2 * at + k, pl.ds(lo, half)], ag_recv.at[t, at])
         if dv == 0:
-            if du == 0:
+            if not early:
+                pass
+            elif du == 0:
                 push(t, at, lo, half, 1, 0)
                 push(t, at, lo, half, -1, 0)
             elif du == 3:
                 push(t, at, lo, quart, 1, 0)
             elif du == 1:
                 push(t, at, lo + quart, quart, -1, 0)
-            push(t, at, lo, half, 0, 1)
-            push(t, at, lo, half, 0, -1)
+            if late:
+                push(t, at, lo, half, 0, 1)
+                push(t, at, lo, half, 0, -1)
         elif dv == 3:
             push(t, at, lo, quart, 0, 1)
         elif dv == 1:
@@ -137,13 +145,16 @@
     normed_v[...] = normed
     inverse_v[...] = inverse
     emb[k] = (normed * gain).astype(BF16)
-    ids[x, y, k] = jnp.concatenate([beam_v[...], pos_v[...]], axis=0).astype(jnp.int16)
-    pl.semaphore_wait(barrier, 1 + 2 * (SIDE - 1) + depth - 1)
-
+    ids[k, c // 2] = jnp.concatenate([beam_v[...], pos_v[...]], axis=0).astype(jnp.int16)
+    pl.semaphore_wait(barrier, SIDE * SIDE + depth - 1)
+
+    def send_ids(i, _):
+        own = ids.at[k, c // 2]
+        copy(own, own, ids_send.at[0], ids_recv.at[0], chip_peer(i)).start()
+        return _
+
+    lax.fori_loop(1, SIDE * SIDE, send_ids, 0)
     event((0, 0), whole=((0, 0),))
-    for i in range(1, SIDE):
-        own = ids.at[x, y, k]
-        copy(own, own, ids_send.at[0], ids_recv.at[0], dev(i, 0)).start()
 
     loads[4].wait()
     wh[...] = (head[...].astype(BF16) * 0.5).astype(BF16)
@@ -153,16 +164,13 @@
     hg[...] = jnp.zeros_like(hg)
     size = size_in[0]
 
-    arrived(ids.at[pl.ds(0, SIDE - 1), y, k], ids_recv.at[0])
-    for i in range(1, SIDE):
-        own = ids.at[:, y, k]
-        copy(own, own, ids_send.at[1], ids_recv.at[1], dev(0, i)).start()
-    event((1, 0), (3, 0))
+    for early in (True, False):
+        for du in (1, 3):
+            for t in range(2):
+                half_in_hand(t, du, 0, early, not early)
+    arrived(ids.at[k, pl.ds(0, SIDE * SIDE - 1)], ids_recv.at[0])
+    copy(ids.at[k], ids.at[k], ids_send.at[1], ids_recv.at[1], sibling).start()
     event((0, 1), (0, 3), whole=((1, 0), (0, 1), (3, 0), (0, 3)))
-    arrived(ids.at[:, pl.ds(0, SIDE - 1), k], ids_recv.at[1])
-    own = ids.at[:, :, k]
-    copy(own, own, ids_send.at[2], ids_recv.at[2], sibling).start()
-
     def chips_of(g):
         first, n = GROUPS[g]
         return range(first, first + n)
@@ -181,7 +189,7 @@
             arrived(emb.at[2 * at + 1 - k], core_recv.at[at])
             dx, dy = CHIPS[at]
             for s in range(2):
-                own = ids[lax.rem(x + dx, SIDE), lax.rem(y + dy, SIDE), s].astype(jnp.int32)
+                own = ids[s, lax.rem(x + dx, SIDE) * SIDE + lax.rem(y + dy, SIDE)].astype(jnp.int32)
                 match = own[0:beam] == c
                 place = lax.broadcasted_iota(jnp.int32, (beam, rows), 0)
                 place = jnp.sum(jnp.where(match, place, 0), axis=0, keepdims=True)
@@ -205,8 +213,10 @@
             slope = jnp.where(slot + 32 * i < limit, slope, 0.0)
             slope_v[pl.ds(32 * i, 32), :many] = slope.astype(BF16)
 
-    def gather_head(g):
-        hg[...] += jnp.dot(slope_of(g), block_of(g), preferred_element_type=F32)
+    def gather_head(g, lo=0, n=width):
+        cols = pl.ds(lo, n)
+        block = emb[pl.ds(2 * GROUPS[g][0], 2 * GROUPS[g][1]), :, cols].reshape(2 * GROUPS[g][1] * rows, n)
+        hg[:, cols] += jnp.dot(slope_of(g), block, preferred_element_type=F32)
 
     def back(g):
         grads = jnp.dot(wt[...], slope_of(g), preferred_element_type=F32).astype(BF16)
@@ -222,7 +232,7 @@
         for at in chips_of(g):
             part[at, k] += from_core[at]
 
-    arrived(ids.at[:, :, k], ids_recv.at[2])
+    arrived(ids.at[1 - k], ids_recv.at[1])
     score(0)
     gather_head(0)
     event((2, 0))
@@ -243,7 +253,6 @@
     event((1, 2), (3, 2), whole=((2, 1), (1, 2), (2, 3), (3, 2)))
     event((2, 2), whole=((2, 2),))
     score(3)
-    gather_head(3)
 
     piece = labels // depth
     part_z = piece // 2
@@ -259,21 +268,28 @@
     def z_first(h):
         hgb[h] = hg[:, h * wide : (h + 1) * wide].astype(BF16)
         for s in range(2):
+            way = 1 - 2 * s
             src = hgb.at[h, rows_z(far, s * part_z, part_z)]
-            copy(src, zq.at[h, s], z_send, z_q.at[h, s], (c, at_z(1 - 2 * s))).start()
-
-    def z_next(h, i):
+            copy(src, zq.at[h, s], z_send, z_q.at[h, s], (c, at_z(way))).start()
         for s in range(2):
             way = 1 - 2 * s
-            own = rows_z(way * (far - 1 - i))
-            if i == 0:
-                arrived(zq.at[h, s], z_q.at[h, s])
-                mid = rows_z(way * (far - 1), s * part_z, part_z)
-                hgb[h, mid] += zq[h, s]
-            else:
-                arrived(zh.at[h, s, i - 1], z_h.at[h, s, i - 1])
-                hgb[h, own] += zh[h, s, i - 1]
-            copy(hgb.at[h, own], zh.at[h, s, i], z_send, z_h.at[h, s, i], (c, at_z(way))).start()
+            copy(hgb.at[h, rows_z(2 * way)], zh.at[h, s, 0], z_send, z_h.at[h, s, 0], (c, at_z(way))).start()
+
+    def z_second(h):
+        for s in range(2):
+            way = 1 - 2 * s
+            arrived(zq.at[h, s], z_q.at[h, s])
+            hgb[h, rows_z(3 * way, s * part_z, part_z)] += zq[h, s]
+            copy(hgb.at[h, rows_z(3 * way)], zh.at[h, s, 1], z_send, z_h.at[h, s, 1], (c, at_z(2 * way))).start()
+
+    def z_third(h):
+        for s in range(2):
+            way = 1 - 2 * s
+            arrived(zh.at[h, s, 0], z_h.at[h, s, 0])
+            arrived(zh.at[h, s, 1], z_h.at[h, s, 1])
+            total = hgb[h, rows_z(way)].astype(F32) + zh[h, s, 0].astype(F32) + zh[h, s, 1].astype(F32)
+            hgb[h, rows_z(way)] = total.astype(BF16)
+            copy(hgb.at[h, rows_z(way)], zh.at[h, s, 2], z_send, z_h.at[h, s, 2], (c, at_z(way))).start()
 
     def adam(h, at):
         cols = pl.ds(h * wide, wide)
@@ -288,21 +304,26 @@
     def z_last(h):
         total = hgb[h, rows_z(0)].astype(F32)
         for s in range(2):
-            arrived(zh.at[h, s, far - 2], z_h.at[h, s, far - 2])
-            total += zh[h, s, far - 2].astype(F32)
+            arrived(zh.at[h, s, 2], z_h.at[h, s, 2])
+            total += zh[h, s, 2].astype(F32)
         hgf[h, rows_z(0)] = total.astype(BF16)
-        for s in range(2):
-            own = hgf.at[h, rows_z(0)]
-            copy(own, own, zg_send, zg.at[h, s, 0], (c, at_z(1 - 2 * s))).start()
-
-    def z_spread(h, i):
+        own = hgf.at[h, rows_z(0)]
+        for i in (2, 1):
+            for s in range(2):
+                copy(own, own, zg_send, zg.at[h, s, i - 1], (c, at_z(i - 2 * i * s))).start()
+
+    def z_spread(h):
         for s in range(2):
             way = 1 - 2 * s
-            own = hgf.at[h, rows_z(-way * i)]
-            arrived(own, zg.at[h, s, i - 1])
-            if i == far - 1:
-                own = hgf.at[h, rows_z(-way * i, s * part_z, part_z)]
-            copy(own, own, zg_send, zg.at[h, s, i], (c, at_z(way))).start()
+            own = hgf.at[h, rows_z(-2 * way)]
+            arrived(own, zg.at[h, s, 1])
+            few = hgf.at[h, rows_z(-2 * way, s * part_z, part_z)]
+            copy(few, few, zg_send, zg.at[h, s, 3], (c, at_z(2 * way))).start()
+            copy(own, own, zg_send, zg.at[h, s, 2], (c, at_z(way))).start()
+
+    def z_came(h, i):
+        for s in range(2):
+            arrived(hgf.at[h, rows_z(2 * i * s - i)], zg.at[h, s, i - 1])
 
     def z_adam(h, i):
         adam(h, rows_z(i))
@@ -310,7 +331,7 @@
 
     def z_end(h):
         for s in range(2):
-            arrived(hgf.at[h, rows_z(far, s * part_z, part_z)], zg.at[h, s, far - 1])
+            arrived(hgf.at[h, rows_z(far, s * part_z, part_z)], zg.at[h, s, 3])
         adam(h, rows_z(far))
 
     fh, fq = width // 2, width // 4
@@ -364,96 +385,91 @@
         egrad[:, t * fh : (t + 1) * fh] = total.T
 
     def g_first():
-        gc[k] = jnp.sum(wh[...].astype(F32) * hg[...], axis=0, keepdims=True) * 2.0
-        copy(gc.at[k], gc.at[k], g_send.at[0], g_recv.at[0], sibling).start()
-
-    def g_x():
-        arrived(gc.at[0], g_recv.at[0])
-        gx[x] = gc[0] + gc[1]
-        for i in range(1, SIDE):
-            copy(gx.at[x], gx.at[x], g_send.at[1], g_recv.at[1], dev(i, 0)).start()
-
-    def g_y():
-        arrived(gx.at[pl.ds(0, SIDE - 1)], g_recv.at[1])
-        gy[y] = jnp.sum(gx[...], axis=0)
-        for i in range(1, SIDE):
-            copy(gy.at[y], gy.at[y], g_send.at[2], g_recv.at[2], dev(0, i)).start()
+        gp[c // 2] = jnp.sum(wh[...].astype(F32) * hg[...], axis=0, keepdims=True) * 2.0
+
+        def send(i, _):
+            own = gp.at[c // 2]
+            copy(own, own, g_send.at[0], g_recv.at[0], chip_peer(i)).start()
+            return _
+
+        lax.fori_loop(1, SIDE * SIDE, send, 0)
+
+    def g_plane():
+        arrived(gp.at[pl.ds(0, SIDE * SIDE - 1)], g_recv.at[0])
+        gc[k] = jnp.sum(gp[...], axis=0)
+        copy(gc.at[k], gc.at[k], g_send.at[1], g_recv.at[1], sibling).start()
 
     def g_z():
-        arrived(gy.at[pl.ds(0, SIDE - 1)], g_recv.at[2])
-        gz[z] = jnp.sum(gy[...], axis=0)
+        arrived(gc.at[0], g_recv.at[1])
+        gz[z] = gc[0] + gc[1]
 
         def send(i, _):
-            copy(gz.at[z], gz.at[z], g_send.at[3], g_recv.at[3], (c, at_z(i))).start()
+            copy(gz.at[z], gz.at[z], g_send.at[2], g_recv.at[2], (c, at_z(i))).start()
             return _
 
         lax.fori_loop(1, depth, send, 0)
 
     def g_last():
-        arrived(gz.at[pl.ds(0, depth - 1)], g_recv.at[3])
+        arrived(gz.at[pl.ds(0, depth - 1)], g_recv.at[2])
         total = jnp.sum(gz[...], axis=0) / gain
         for i in range(width // 128):
             ggrad_ref[i : i + 1, :] = total[:, i * 128 : (i + 1) * 128]
 
     chunks = range(ZC)
     for h in chunks:
+        gather_head(3, h * wide, wide)
         z_first(h)
+    for t in range(2):
+        v_first(t, 0)
+    g_first()
     back(3)
     join(2)
-    g_first()
-    for h in chunks:
-        z_next(h, 0)
+    for h in chunks:
+        z_second(h)
     join(3)
-    for du in (2, 1, 3, 0):
+    for du in (2, 1, 3):
         for t in range(2):
             v_first(t, du)
-    g_x()
-    for h in chunks:
-        z_next(h, 1)
-    for t in range(2):
-        v_next(t, 2)
-    for t in range(2):
-        v_next(t, 1)
-    for h in chunks[: ZC // 2]:
-        z_next(h, 2)
+    for t in range(2):
+        v_next(t, 0)
+    for h in chunks:
+        z_third(h)
+    for du in (2, 1):
+        for t in range(2):
+            v_next(t, du)
+    g_plane()
     for t in range(2):
         v_next(t, 3)
-    for h in chunks[ZC // 2 :]:
-        z_next(h, 2)
-    for t in range(2):
-        v_next(t, 0)
-    g_y()
-    for h in chunks[: ZC // 2]:
+    for h in chunks:
         z_last(h)
+    g_z()
+    loads[5].wait()
+    loads[6].wait()
     for t in range(2):
         v_last(t, 2)
         u_first(t)
-    for h in chunks[ZC // 2 :]:
-        z_last(h)
-    loads[5].wait()
-    loads[6].wait()
+    for h in chunks:
+        adam(h, rows_z(0))
+    for h in chunks:
+        z_spread(h)
     for t in range(2):
         v_last(t, 1)
-    for h in chunks:
-        z_spread(h, 1)
-    g_z()
     for t in range(2):
         v_last(t, 3)
     for t in range(2):
         u_next(t)
     for h in chunks:
-        z_spread(h, 2)
-        adam(h, rows_z(0))
+        z_came(h, 1)
+        z_adam(h, 1)
     for t in range(2):
         v_last(t, 0)
     for h in chunks:
-        z_adam(h, 1)
-    for h in chunks:
-        z_spread(h, 3)
+        z_adam(h, 2)
+    for h in chunks:
+        z_came(h, 3)
+        z_adam(h, 3)
     for t in range(2):
         u_last(t)
-    for h in chunks:
-        z_adam(h, 2)
 
     scaled = egrad[...] * gain
     normed = normed_v[...]
@@ -461,8 +477,6 @@
     second_mean = jnp.mean(scaled * normed, axis=1, keepdims=True)
     igrad_ref[...] = ((scaled - first_mean - normed * second_mean) * inverse_v[...]).astype(BF16)
 
-    for h in chunks:
-        z_adam(h, 3)
     g_last()
     for h in chunks:
         z_end(h)
@@ -470,13 +484,11 @@
     sent(emb.at[pl.ds(0, PLANE - 1)], ag_send)
     sent(from_core, core_send)
     sent(from_core.at[pl.ds(0, PLANE // 2 - 1)], rs_send)
-    sent(ids.at[pl.ds(0, SIDE - 1), y, k], ids_send.at[0])
-    sent(ids.at[:, pl.ds(0, SIDE - 1), k], ids_send.at[1])
-    sent(ids.at[:, :, k], ids_send.at[2])
-    sent(gc.at[0], g_send.at[0])
-    sent(gx.at[pl.ds(0, SIDE - 1)], g_send.at[1])
-    sent(gy.at[pl.ds(0, SIDE - 1)], g_send.at[2])
-    sent(gz.at[pl.ds(0, depth - 1)], g_send.at[3])
+    sent(ids.at[k, pl.ds(0, SIDE * SIDE - 1)], ids_send.at[0])
+    sent(ids.at[k], ids_send.at[1])
+    sent(gp.at[pl.ds(0, SIDE * SIDE - 1)], g_send.at[0])
+    sent(gc.at[0], g_send.at[1])
+    sent(gz.at[pl.ds(0, depth - 1)], g_send.at[2])
     sent(hgb.at[:, pl.ds(0, labels - piece)], z_send)
     sent(hgf.at[:, pl.ds(0, labels - piece)], zg_send)
 
@@ -529,7 +541,7 @@
             pltpu.VMEM((labels, width), F32),
             pltpu.VMEM((labels, width), F32),
             pltpu.VMEM((PLANE, rows, width), BF16),
-            pltpu.VMEM((SIDE, SIDE, 2, beam + pos, rows), jnp.int16),
+            pltpu.VMEM((2, SIDE * SIDE, beam + pos, rows), jnp.int16),
             pltpu.VMEM((labels, width), BF16),
             pltpu.VMEM((width, labels), BF16),
             pltpu.VMEM((labels, width), F32),
@@ -543,17 +555,16 @@
             pltpu.VMEM((ZC, labels, wide), BF16),
             pltpu.VMEM((ZC, labels, wide), BF16),
             pltpu.VMEM((ZC, 2, piece // 2, wide), BF16),
-            pltpu.VMEM((ZC, 2, far - 1, piece, wide), BF16),
+            pltpu.VMEM((ZC, 2, 3, piece, wide), BF16),
+            pltpu.VMEM((SIDE * SIDE, 1, width), F32),
             pltpu.VMEM((2, 1, width), F32),
-            pltpu.VMEM((SIDE, 1, width), F32),
-            pltpu.VMEM((SIDE, 1, width), F32),
             pltpu.VMEM((depth, 1, width), F32),
             pltpu.VMEM((rows, width), F32),
             pltpu.VMEM((rows, width), F32),
             pltpu.VMEM((rows, 1), F32),
             dma((7,)),
-            dma((3,)),
-            dma((3,)),
+            dma((2,)),
+            dma((2,)),
             dma,
             dma((2, len(CHIPS))),
             dma((len(CHIPS),)),
@@ -566,11 +577,11 @@
             dma((2, 2)),
             dma,
             dma((ZC, 2)),
-            dma((ZC, 2, far - 1)),
+            dma((ZC, 2, 3)),
             dma,
-            dma((ZC, 2, far)),
-            dma((4,)),
-            dma((4,)),
+            dma((ZC, 2, 4)),
+            dma((3,)),
+            dma((3,)),
         ],
         compiler_params=pltpu.CompilerParams(
             collective_id=0, has_side_effects=True, vmem_limit_bytes=48 * 1024 * 1024

time: 72.8 us -> 69.6 us (0.956)
  Pallas kernels: 70.4 us -> 67.6 us
    pallas_call x1, Pallas kernels: 68.1 us -> 65.3 us  [shards(): pl.pallas_call(kernel, out_shape=(head_shape, head_shape, head_shape, plt...]
where the time goes in v5:
time: 69.6 us; the launch traced here: 69 us
  Pallas kernels  67.6 us (97%)
  between operations  1.45 us (2%)
    pallas_call x1, Pallas kernels, shards(): pl.pallas_call(kernel, out_shape=(head_shape, head_shape, head_shape, plt...  65.3 us
    pallas_call x1, Pallas kernels, shards(): pl.pallas_call(store, out_shape=(whole, whole, whole, *[pltpu.HBM(r.shape...  2.28 us

profile of v5, /device:TPU:2, one launch (start us, length us, event | category | flops | bytes accessed | tf_op | source)
XLA Modules:
  0.0 69.0 jit_solution(14112318409411281618)
XLA Ops:
  1.3 65.3 %shard_map.119 = (f32[512,768]{1,0:T(8,128)S(1)}, f32[512,768]{1,0:T(8,128)S(1)}, f32[512,768]{1,0:T(8,128)S(1)}, bf16[128,768]{1,0:T(8,128)(2,1)S(1)}, f32[6,128]{1,0:T(8,128)S(1)}) custom-call(s32[1]{0:T(128)S(6)} %copy.13.size_in, bf16[128,768]{1,0:T(8,128)(2,1)} %hid_in.1, f32[6,128]{1,0:T(8,128)} %bitcast.10, s32[8,128]{1,0:T(8,128)} %bitcast.11, ...), custom_call_target="tpu_custom_call" | custom-call | tf_op jit(solution)/shard_map/pallas_call | solution.py:524
  66.6 2.3 %shard_map.120 = (f32[1,512,768]{2,1,0:T(8,128)}, f32[1,512,768]{2,1,0:T(8,128)}, f32[1,512,768]{2,1,0:T(8,128)}, bf16[128,768]{1,0:T(8,128)(2,1)}, f32[6,128]{1,0:T(8,128)}) custom-call(f32[512,768]{1,0:T(8,128)S(1)} %get-tuple-element.15.nh, f32[512,768]{1,0:T(8,128)S(1)} %get-tuple-element.16.nf, f32[512,768]{1,0:T(8,128)S(1)} %get-tuple-element.17.ns, ...), custom_call_target="tpu_custom_call" | custom-call | tf_op jit(solution)/shard_map/pallas_call | solution.py:600

commit v6 on v5

--- a/solution.py
+++ b/solution.py
@@ -27,7 +27,7 @@
 PLACE = {offset: i for i, offset in enumerate(CHIPS)}
 GROUPS = ((0, 5), (5, 3), (8, 3), (11, 5))
 MOST = max(n for _, n in GROUPS)
-ZC = 3
+ZC = 2
 
 
 def kernel(
@@ -423,9 +423,9 @@
         v_first(t, 0)
     g_first()
     back(3)
+    for h in chunks:
+        z_second(h)
     join(2)
-    for h in chunks:
-        z_second(h)
     join(3)
     for du in (2, 1, 3):
         for t in range(2):

time: 69.6 us -> 68.8 us (0.989)
  Pallas kernels: 67.6 us -> 66.1 us
    pallas_call x1, Pallas kernels: 65.3 us -> 63.8 us  [shards(): pl.pallas_call(kernel, out_shape=(head_shape, head_shape, head_shape, plt...]
where the time goes in v6:
time: 68.8 us; the launch traced here: 67.5 us
  Pallas kernels  66.1 us (96%)
  between operations  1.45 us (2%)
    pallas_call x1, Pallas kernels, shards(): pl.pallas_call(kernel, out_shape=(head_shape, head_shape, head_shape, plt...  63.8 us
    pallas_call x1, Pallas kernels, shards(): pl.pallas_call(store, out_shape=(whole, whole, whole, *[pltpu.HBM(r.shape...  2.28 us

profile of v6, /device:TPU:2, one launch (start us, length us, event | category | flops | bytes accessed | tf_op | source)
XLA Modules:
  0.0 67.5 jit_solution(3494730544008526152)
XLA Ops:
  1.3 63.8 %shard_map.119 = (f32[512,768]{1,0:T(8,128)S(1)}, f32[512,768]{1,0:T(8,128)S(1)}, f32[512,768]{1,0:T(8,128)S(1)}, bf16[128,768]{1,0:T(8,128)(2,1)S(1)}, f32[6,128]{1,0:T(8,128)S(1)}) custom-call(s32[1]{0:T(128)S(6)} %copy.13.size_in, bf16[128,768]{1,0:T(8,128)(2,1)} %hid_in.1, f32[6,128]{1,0:T(8,128)} %bitcast.10, s32[8,128]{1,0:T(8,128)} %bitcast.11, ...), custom_call_target="tpu_custom_call" | custom-call | tf_op jit(solution)/shard_map/pallas_call | solution.py:524
  65.1 2.3 %shard_map.120 = (f32[1,512,768]{2,1,0:T(8,128)}, f32[1,512,768]{2,1,0:T(8,128)}, f32[1,512,768]{2,1,0:T(8,128)}, bf16[128,768]{1,0:T(8,128)(2,1)}, f32[6,128]{1,0:T(8,128)}) custom-call(f32[512,768]{1,0:T(8,128)S(1)} %get-tuple-element.15.nh, f32[512,768]{1,0:T(8,128)S(1)} %get-tuple-element.16.nf, f32[512,768]{1,0:T(8,128)S(1)} %get-tuple-element.17.ns, ...), custom_call_target="tpu_custom_call" | custom-call | tf_op jit(solution)/shard_map/pallas_call | solution.py:600
